TPU v7x, 128 devices: a whole 4x4x4 slice. The times are simulated.
128 devices in a mesh: ctx: 8 (over y, x_lo), grp: 16 (over z, x_hi, core).
Axes of the slice: x: 4 (x_hi: 2, x_lo: 2; x = x_hi * 2 + x_lo), y: 4, z: 4, core: 2. Of those that a mesh axis runs over, the one named last changes fastest.
Arguments:
- features: bfloat16 [3, 4096, 8192], P(None, 'ctx', 'grp'), may hold values from -6 to 6
- short_weight: float32 [3, 3, 8192], P(None, None, 'grp'), may hold values from -3 to 3
- long_filter: bfloat16 [4096, 8192], P('ctx', 'grp'), may hold values from -0.1875 to 0.1875
- lengths: int32 [32], replicated, may hold values from 128 to 4096, as said below
- skip_gain: float32 [8192], P('grp'), may hold values from 0.5 to 1.5
- out_weight: bfloat16 [8192, 8192], P('grp'), may hold values from -0.0625 to 0.0625
Outputs:
- mixed: bfloat16 [4096, 8192], P('ctx', 'grp')
Inputs may be any that keep to these rules, and one draw needn't show every extreme that they name: `lengths`: every length is a multiple of 128; some group has length 4096 and some group has length 128.
All inputs are finite; a program needn't handle non-finite values.
Results may differ from a plain program's by a relative error of at most 0.0049.
Values may be sent and summed in bfloat16 or wider, within the bound.
A program may use at most 192 MiB of HBM per device.

v0:
```python
import math

import jax
import jax.numpy as jnp
from jax import lax
from jax.sharding import PartitionSpec as P

GROUP_CH = 256


def from_behind(value, axis, steps):
    count = lax.axis_size(axis)
    first, last = (max(0, -steps), min(count, count - steps))
    return lax.ppermute(value, axis, [(source, source + steps) for source in range(first, last)])


def tables(span):
    period = 2 * span
    freqs = span + 1
    fidx = jnp.arange(freqs, dtype=jnp.int32)[:, None]
    nidx = jnp.arange(span, dtype=jnp.int32)[None, :]
    angle = (fidx * nidx % period).astype(jnp.float32) * (2.0 * math.pi / period)
    forward = jnp.concatenate([jnp.cos(angle), -jnp.sin(angle)], axis=0)
    tindex = jnp.arange(period, dtype=jnp.int32)[:, None]
    findex = jnp.arange(freqs, dtype=jnp.int32)[None, :]
    angle_back = (tindex * findex % period).astype(jnp.float32) * (2.0 * math.pi / period)
    weight = jnp.where((findex == 0) | (findex == span), 1.0, 2.0).astype(jnp.float32) / period
    inverse = jnp.concatenate([weight * jnp.cos(angle_back), -weight * jnp.sin(angle_back)], axis=1)
    return (forward, inverse)


def transform(forward, block):
    return jnp.dot(
        forward, block, precision=lax.Precision.HIGHEST, preferred_element_type=jnp.float32
    )


def product_back(inverse, sig_spec, fil_spec, freqs):
    sig_re, sig_im = (sig_spec[:freqs], sig_spec[freqs:])
    fil_re, fil_im = (fil_spec[:freqs], fil_spec[freqs:])
    stacked = jnp.concatenate(
        [sig_re * fil_re - sig_im * fil_im, sig_re * fil_im + sig_im * fil_re], axis=0
    )
    return jnp.dot(
        inverse, stacked, precision=lax.Precision.HIGHEST, preferred_element_type=jnp.float32
    )


def per_device(features, short_weight, long_filter, lengths, skip_gain, out_weight):
    span = features.shape[1]
    width = features.shape[2]
    nctx = lax.axis_size("ctx")
    freqs = span + 1
    rims_prev = from_behind(features[:, span - 2 :, :], "ctx", 1)
    extended = jnp.concatenate([rims_prev, features], axis=1).astype(jnp.float32)
    short = short_weight[0][:, None, :] * extended[:, 2:, :]
    short = short + short_weight[1][:, None, :] * extended[:, 1:-1, :]
    short = short + short_weight[2][:, None, :] * extended[:, :-2, :]
    query = short[0]
    signal = short[1] * short[2]
    groups_dev = width // GROUP_CH
    group_start = lax.axis_index("grp") * groups_dev
    local_len = lax.dynamic_slice(lengths, (group_start,), (groups_dev,))
    chan_len = jnp.repeat(local_len, GROUP_CH)
    longest = jnp.max(local_len)
    offsets = jnp.arange(span, dtype=jnp.int32)
    forward, inverse = tables(span)
    sig_spec = transform(forward, signal)
    all_taps = lax.all_gather(long_filter, "ctx", axis=0, tiled=True)
    blank = jnp.zeros((2 * span, width), jnp.float32)
    tail = jnp.zeros((span, width), jnp.float32)
    partials = []
    for dist in range(nctx):

        def build(unused, dist=dist):
            taps = all_taps[dist * span : (dist + 1) * span].astype(jnp.float32)
            pos = dist * span + offsets
            cut = jnp.where(pos[:, None] < chan_len[None, :], taps, jnp.float32(0.0))
            return product_back(inverse, sig_spec, transform(forward, cut), freqs)

        window = lax.cond(dist * span < longest, build, lambda unused: blank, 0)
        partials.append(window[:span] + tail)
        tail = window[span:]
    here = lax.axis_index("ctx")
    buffer = jnp.zeros((2 * nctx * span, width), jnp.float32)
    for dist in range(nctx):
        buffer = lax.dynamic_update_slice_in_dim(buffer, partials[dist], (here + dist) * span, 0)
    conv = lax.psum_scatter(buffer[: nctx * span], "ctx", scatter_dimension=0, tiled=True)
    gated = (query * (conv + skip_gain[None, :] * signal)).astype(jnp.bfloat16)
    projected = jnp.dot(gated, out_weight, preferred_element_type=jnp.float32)
    return lax.psum_scatter(projected, "grp", scatter_dimension=1, tiled=True).astype(jnp.bfloat16)


def solution(mesh):
    return jax.shard_map(
        per_device,
        mesh=mesh,
        in_specs=(
            P(None, "ctx", "grp"),
            P(None, None, "grp"),
            P("ctx", "grp"),
            P(),
            P("grp"),
            P("grp", None),
        ),
        out_specs=P("ctx", "grp"),
        check_vma=False,
    )
```

profile of v0, /device:TPU:0, one launch (start us, length us, event | category | flops | bytes accessed | tf_op | source)
XLA Modules:
  0.0 669.1 jit_solution(7917156607760599823)
XLA Ops:
  6.5 0.7 all-gather.2.cloned.1.call-update
  7.3 0.8 slice.218
  8.1 3.5 collective-permute-start
  11.6 4.2 sine_negate_fusion
  16.0 10.8 %sine_multiply_fusion = (f32[1024,513]{1,0:T(8,128)S(1)}, f32[1024,513]{1,0:T(8,128)S(1)}) fusion(f32[513]{0:T(1024)S(1)} %fusion.153, f32[513]{0:T(1024)S(1)} %select_multiply_fusion), kind=kLoop, calls=%fused_computation.155 | loop fusion | flops 8404992 | bytes 4206600 | tf_op jit(solution)/shard_map/mul | solution.py:28
  26.9 3.0 pad_maximum_fusion
  29.8 0.7 fusion.154
  35.8 1.9 maximum_convert_fusion
  37.7 0.9 fusion.128
  38.6 1.6 copy-done.8
  40.2 4.8 fusion.150
  45.1 57.2 %all-gather.2.cloned.1.call-done = bf16[4096,512]{1,0:T(8,128)(2,1)} async-done(((bf16[512,512]{1,0:T(8,128)(2,1)}), bf16[4096,512]{1,0:T(8,128)(2,1)}) %all-gather.2.cloned.1.call-update) | async-done | bytes 4194320 | tf_op jit(solution)/shard_map/all_gather | solution.py:69
  102.3 26.2 %conditional.8 = (f32[512,512]{0,1:T(8,128)}, f32[512,512]{1,0:T(8,128)S(1)}) conditional(s32[]{:T(128)} %convert_element_type.69, () %tuple.63, (f32[1026,512]{1,0:T(8,128)}, s32[512]{0:T(512)S(1)}, s32[2,256]{1,0:T(2,128)S(1)}, bf16[4096,512]{1,0:T(8,128)(2,1)}, f32[1026,512]{1,0:T(8,128)S(1)}, /*index=5*/f32[1024,1026]{1,0:T(8,128)}) %tuple.64), branch_computations={%region_1.2_spmd, %region_2.3_spmd} | conditional | flops 9685438464 | bytes 50946120 | solution.py:81
  102.5 4.9 convolution_bitcast_fusion
  107.5 0.5 multiply_subtract_fusion
  108.0 1.8 copy-done.10
  109.8 15.2 %fusion.4 = f32[1024,512]{0,1:T(8,128)S(1)} fusion(f32[1024,1026]{1,0:T(8,128)S(1)} %copy-done.10, f32[513,512]{1,0:T(8,128)S(1)} %get-tuple-element.192, f32[513,512]{1,0:T(8,128)S(1)} %get-tuple-element.191), kind=kOutput, calls=%fused_computation.5 | convolution fusion | flops 6455559168 | bytes 8400896 | tf_op jit(solution)/shard_map/cond/branch_1_fun/dot_general | solution.py:44
  125.0 1.5 fusion.155
  126.6 1.6 copy.16
  128.5 1.0 copy-done.22
  129.5 24.0 %conditional.10 = (f32[1024,512]{0,1:T(8,128)}) conditional(s32[]{:T(128)} %convert_element_type.73, () %tuple.66, (f32[1026,512]{1,0:T(8,128)}, s32[512]{0:T(512)S(1)}, s32[2,256]{1,0:T(2,128)S(1)}, bf16[4096,512]{1,0:T(8,128)(2,1)}, f32[1026,512]{1,0:T(8,128)S(1)}, /*index=5*/f32[1024,1026]{1,0:T(8,128)}) %tuple.64), branch_computations={%region_5.6_spmd, %region_6.7_spmd} | conditional | flops 9685438464 | bytes 44658752 | solution.py:81
  129.5 4.9 convolution_bitcast_fusion.2
  134.5 0.5 multiply_subtract_fusion.2
  135.0 1.8 copy-done.11
  136.8 16.5 %fusion.36 = f32[1024,512]{0,1:T(8,128)} fusion(f32[1024,1026]{1,0:T(8,128)S(1)} %copy-done.11, f32[513,512]{1,0:T(8,128)S(1)} %get-tuple-element.198, f32[513,512]{1,0:T(8,128)S(1)} %get-tuple-element.197), kind=kOutput, calls=%fused_computation.40 | convolution fusion | flops 6455559168 | bytes 8400896 | tf_op jit(solution)/shard_map/cond/branch_1_fun/dot_general | solution.py:44
  153.5 24.2 %conditional.11 = (f32[1024,512]{0,1:T(8,128)}) conditional(s32[]{:T(128)} %convert_element_type.74, () %tuple.67, (f32[1026,512]{1,0:T(8,128)}, s32[512]{0:T(512)S(1)}, s32[2,256]{1,0:T(2,128)S(1)}, bf16[4096,512]{1,0:T(8,128)(2,1)}, f32[1026,512]{1,0:T(8,128)S(1)}, /*index=5*/f32[1024,1026]{1,0:T(8,128)}) %tuple.64), branch_computations={%region_7.8_spmd, %region_8.9_spmd} | conditional | flops 9685438464 | bytes 44658752 | solution.py:81
  153.6 4.9 convolution_bitcast_fusion.3
  159.1 1.8 copy-done.12
  160.9 16.7 %fusion.52 = f32[1024,512]{0,1:T(8,128)} fusion(f32[1024,1026]{1,0:T(8,128)S(1)} %copy-done.12, f32[513,512]{1,0:T(8,128)S(1)} %get-tuple-element.200, f32[513,512]{1,0:T(8,128)S(1)} %get-tuple-element.199), kind=kOutput, calls=%fused_computation.58 | convolution fusion | flops 6455559168 | bytes 8400896 | tf_op jit(solution)/shard_map/cond/branch_1_fun/dot_general | solution.py:44
  177.7 24.3 %conditional.12 = (f32[1024,512]{0,1:T(8,128)}) conditional(s32[]{:T(128)} %convert_element_type.75, () %tuple.68, (f32[1026,512]{1,0:T(8,128)}, s32[512]{0:T(512)S(1)}, s32[2,256]{1,0:T(2,128)S(1)}, bf16[4096,512]{1,0:T(8,128)(2,1)}, f32[1026,512]{1,0:T(8,128)S(1)}, /*index=5*/f32[1024,1026]{1,0:T(8,128)}) %tuple.64), branch_computations={%region_9.10_spmd, %region_10.11_spmd} | conditional | flops 9685438464 | bytes 44658752 | solution.py:81
  177.8 4.9 convolution_bitcast_fusion.4
  183.3 1.8 copy-done.13
  185.1 16.6 %fusion.68 = f32[1024,512]{0,1:T(8,128)} fusion(f32[1024,1026]{1,0:T(8,128)S(1)} %copy-done.13, f32[513,512]{1,0:T(8,128)S(1)} %get-tuple-element.202, f32[513,512]{1,0:T(8,128)S(1)} %get-tuple-element.201), kind=kOutput, calls=%fused_computation.76 | convolution fusion | flops 6455559168 | bytes 8400896 | tf_op jit(solution)/shard_map/cond/branch_1_fun/dot_general | solution.py:44
  202.1 24.1 %conditional.13 = (f32[1024,512]{0,1:T(8,128)}) conditional(s32[]{:T(128)} %convert_element_type.76, () %tuple.69, (f32[1026,512]{1,0:T(8,128)}, s32[512]{0:T(512)S(1)}, s32[2,256]{1,0:T(2,128)S(1)}, bf16[4096,512]{1,0:T(8,128)(2,1)}, f32[1026,512]{1,0:T(8,128)S(1)}, /*index=5*/f32[1024,1026]{1,0:T(8,128)}) %tuple.64), branch_computations={%region_11.12_spmd, %region_12.13_spmd} | conditional | flops 9685438464 | bytes 44658752 | solution.py:81
  202.1 4.9 convolution_bitcast_fusion.5
  207.6 1.8 copy-done.14
  209.4 16.5 %fusion.84 = f32[1024,512]{0,1:T(8,128)} fusion(f32[1024,1026]{1,0:T(8,128)S(1)} %copy-done.14, f32[513,512]{1,0:T(8,128)S(1)} %get-tuple-element.204, f32[513,512]{1,0:T(8,128)S(1)} %get-tuple-element.203), kind=kOutput, calls=%fused_computation.94 | convolution fusion | flops 6455559168 | bytes 8400896 | tf_op jit(solution)/shard_map/cond/branch_1_fun/dot_general | solution.py:44
  226.2 24.3 %conditional.14 = (f32[1024,512]{0,1:T(8,128)}) conditional(s32[]{:T(128)} %convert_element_type.77, () %tuple.70, (f32[1026,512]{1,0:T(8,128)}, s32[512]{0:T(512)S(1)}, s32[2,256]{1,0:T(2,128)S(1)}, bf16[4096,512]{1,0:T(8,128)(2,1)}, f32[1026,512]{1,0:T(8,128)S(1)}, /*index=5*/f32[1024,1026]{1,0:T(8,128)}) %tuple.64), branch_computations={%region_13.14_spmd, %region_14.15_spmd} | conditional | flops 9685438464 | bytes 44658752 | solution.py:81
  226.2 4.9 convolution_bitcast_fusion.6
  231.7 1.8 copy-done.15
  233.5 16.8 %fusion.100 = f32[1024,512]{0,1:T(8,128)} fusion(f32[1024,1026]{1,0:T(8,128)S(1)} %copy-done.15, f32[513,512]{1,0:T(8,128)S(1)} %get-tuple-element.206, f32[513,512]{1,0:T(8,128)S(1)} %get-tuple-element.205), kind=kOutput, calls=%fused_computation.112 | convolution fusion | flops 6455559168 | bytes 8400896 | tf_op jit(solution)/shard_map/cond/branch_1_fun/dot_general | solution.py:44
  250.5 24.3 %conditional.9 = (f32[1024,512]{0,1:T(8,128)}) conditional(s32[]{:T(128)} %convert_element_type.72, () %tuple.65, (f32[1026,512]{1,0:T(8,128)}, s32[512]{0:T(512)S(1)}, s32[2,256]{1,0:T(2,128)S(1)}, bf16[4096,512]{1,0:T(8,128)(2,1)}, f32[1026,512]{1,0:T(8,128)S(1)}, /*index=5*/f32[1024,1026]{1,0:T(8,128)}) %tuple.64), branch_computations={%region_3.4_spmd, %region_4.5_spmd} | conditional | flops 9685438464 | bytes 44658752 | solution.py:81
  250.5 4.9 convolution_bitcast_fusion.1
  256.0 1.8 copy-done.16
  257.8 16.5 %fusion.20 = f32[1024,512]{0,1:T(8,128)} fusion(f32[1024,1026]{1,0:T(8,128)S(1)} %copy-done.16, f32[513,512]{1,0:T(8,128)S(1)} %get-tuple-element.196, f32[513,512]{1,0:T(8,128)S(1)} %get-tuple-element.195), kind=kOutput, calls=%fused_computation.22 | convolution fusion | flops 6455559168 | bytes 8400896 | tf_op jit(solution)/shard_map/cond/branch_1_fun/dot_general | solution.py:44
  274.7 22.9 %conditional.15 = (f32[512,512]{0,1:T(8,128)S(1)}) conditional(s32[]{:T(128)} %convert_element_type.78, () %tuple.71, (f32[1026,512]{1,0:T(8,128)}, s32[512]{0:T(512)S(1)}, s32[2,256]{1,0:T(2,128)S(1)}, bf16[4096,512]{1,0:T(8,128)(2,1)}, f32[1026,512]{1,0:T(8,128)S(1)}, /*index=5*/f32[1024,1026]{1,0:T(8,128)}) %tuple.64), branch_computations={%region_15.16_spmd, %region_16.17_spmd} | conditional | flops 9685438464 | bytes 46755904 | solution.py:81
  274.8 4.9 convolution_bitcast_fusion.7
  280.3 1.8 copy-done.17
  282.1 15.2 %fusion.116 = f32[1024,512]{0,1:T(8,128)S(1)} fusion(f32[1024,1026]{1,0:T(8,128)S(1)} %copy-done.17, f32[513,512]{1,0:T(8,128)S(1)} %get-tuple-element.208, f32[513,512]{1,0:T(8,128)S(1)} %get-tuple-element.207), kind=kOutput, calls=%fused_computation.130 | convolution fusion | flops 6455559168 | bytes 8400896 | tf_op jit(solution)/shard_map/cond/branch_1_fun/dot_general | solution.py:44
  297.6 1.0 copy-done.24
  298.6 8.9 %slice_add_fusion = (f32[512,512]{0,1:T(8,128)}, f32[512,512]{0,1:T(8,128)S(1)}, f32[512,512]{0,1:T(8,128)S(1)}, f32[512,512]{0,1:T(8,128)S(1)}, f32[512,512]{0,...) fusion(f32[512,512]{0,1:T(8,128)} %copy-done.24, f32[1024,512]{0,1:T(8,128)} %get-tuple-element.232, ...), kind=kLoop, calls=%fused_computation.172 | loop fusion | flops 1835008 | bytes 22020096 | tf_op jit(solution)/shard_map/add | solution.py:82
  307.5 2.5 copy.8
  310.0 2.5 copy.9
  312.6 2.6 copy.10
  315.1 1.3 copy.11
  317.1 1.6 copy.14
  318.7 2.1 broadcast_in_dim.74
  321.0 1.1 copy-done.21
  322.5 0.9 copy-done.19
  324.0 4.3 slice.277
  328.4 169.2 %reduce-scatter.3.cloned.1.call-done = f32[512,512]{1,0:T(8,128)} async-done(((f32[4096,512]{1,0:T(8,128)}), f32[512,512]{1,0:T(8,128)}) %reduce-scatter.3.cloned.1.call-update) | async-done | bytes 1048592 | tf_op jit(solution)/shard_map/reduce_scatter | solution.py:88
  497.5 14.1 %fusion.146 = f32[512,8192]{1,0:T(8,128)} fusion(bf16[512,8192]{1,0:T(8,128)(2,1)} %param.27, f32[3,512,512]{2,1,0:T(8,128)S(1)} %copy-done.9, f32[512,512]{1,0:T(8,128)} %reduce-scatter.3.cloned.1.call-done, f32[512]{0:T(512)S(1)} %copy-done.25), kind=kOutput, calls=%fused_computation.185 | convolution fusion | flops 4296278016 | bytes 29362176 | tf_op jit(solution)/shard_map/dot_general | solution.py:90
  511.6 148.6 %reduce-scatter.5.cloned.1.call-done = f32[512,512]{1,0:T(8,128)} async-done(((f32[512,8192]{1,0:T(8,128)}), f32[512,512]{1,0:T(8,128)}) %reduce-scatter.5.cloned.1.call-update) | async-done | bytes 1048592 | tf_op jit(solution)/shard_map/reduce_scatter | solution.py:91
  660.2 2.1 convert_element_type.80
  (87 shorter events, 5.6 us)
Async XLA Ops:
  6.5 9.2 %copy-start.26 = (f32[3,3,512]{2,1,0:T(4,128)S(1)}, f32[3,3,512]{2,1,0:T(4,128)}, u32[]{:S(2)}) copy-start(f32[3,3,512]{2,1,0:T(4,128)} %param.23) | copy-start | bytes 55300
  6.5 95.7 %all-gather.2.cloned.1.call-start = ((), (), s32[]{:S(2)}) async-start(), calls=%async_computation.2 | async-start | bytes 4718592 | tf_op jit(solution)/shard_map/all_gather | solution.py:69
  7.3 490.3 %reduce-scatter.3.cloned.1.call-start = ((), (), s32[]{:S(2)}) async-start(), calls=%async_computation.3 | async-start | bytes 9437184 | tf_op jit(solution)/shard_map/reduce_scatter | solution.py:88
  8.1 27.7 %collective-permute-start = (bf16[3,2,512]{2,1,0:T(2,128)(2,1)S(1)}, bf16[3,2,512]{2,1,0:T(2,128)(2,1)S(1)}, u32[]{:S(2)}, u32[]{:S(2)}) collective-permute-start(bf16[3,2,512]{2,1,0:T(2,128)(2,1)S(1)} %slice.218), channel_id=1, source_target_pairs={{0,16},{16,32},{32,48},{48,64},{64,80},{80,96},{96,112},{1,17},{17... | collective-permute-start | bytes 18440 | tf_op jit(solution)/shard_map/ppermute | solution.py:14
  26.9 3.0 copy-start.27
  38.6 1.7 copy-start.8
  102.5 5.0 copy-start
  107.5 2.3 copy-start.10
  128.5 1.0 copy-start.22
  129.5 5.0 copy-start.1
  134.5 2.3 copy-start.11
  153.6 5.0 copy-start.2
  158.5 2.3 copy-start.12
  177.8 5.0 copy-start.3
  182.8 2.3 copy-start.13
  202.1 5.0 copy-start.4
  207.1 2.3 copy-start.14
  226.2 5.0 copy-start.5
  231.2 2.3 copy-start.15
  250.5 5.0 copy-start.6
  255.5 2.3 copy-start.16
  274.8 5.0 copy-start.7
  279.8 2.3 copy-start.17
  297.6 1.0 copy-start.24
  318.7 2.2 copy-start.23
  320.8 1.2 copy-start.21
  320.9 1.5 copy-start.20
  322.1 1.3 copy-start.19
  322.4 1.3 copy-start.18
  328.3 169.3 %copy-start.9 = (f32[3,512,512]{2,1,0:T(8,128)S(1)}, f32[3,512,512]{2,1,0:T(8,128)}, u32[]{:S(2)}) copy-start(f32[3,512,512]{2,1,0:T(8,128)} %copy-done.8) | copy-start | bytes 9437188
  328.3 169.3 %copy-start.25 = (f32[512]{0:T(512)S(1)}, f32[512]{0:T(512)}, u32[]{:S(2)}) copy-start(f32[512]{0:T(512)} %param.26) | copy-start | bytes 6148
  328.3 331.9 %reduce-scatter.5.cloned.1.call-start = ((), (), s32[]{:S(2)}) async-start(), calls=%async_computation.4 | async-start | bytes 17825792 | tf_op jit(solution)/shard_map/reduce_scatter | solution.py:91
Sparse Core Ops, SparseCore 0:
  9.0 93.1 all-gather.1
  328.4 169.0 reduce-scatter.2
  511.8 148.4 reduce-scatter.4
where the time goes:
time: 679 us; the launch traced here: 669 us
  waiting for transfers between devices  376 us (55%)
  matrix products  189 us (28%)
  local copies, waits for them, and re-layouts  42.7 us (6%)
  other arithmetic  37 us (5%)
  between operations  18.8 us (3%)
    reduce_scatter x1, waiting for transfers between devices, per_device(): lax.psum_scatter(buffer[:nctx * span], 'ctx', scatter_dimension=0, tiled=...  169 us
    reduce_scatter x1, waiting for transfers between devices, per_device(): lax.psum_scatter(projected, 'grp', scatter_dimension=1, tiled=True)  149 us
    dot_general x8, matrix products, product_back(): jnp.dot(inverse, stacked, precision=lax.Precision.HIGHEST, preferred_elem...  130 us
    all_gather x1, waiting for transfers between devices, per_device(): all_taps = lax.all_gather(long_filter, 'ctx', axis=0, tiled=True)  57.2 us
    dot_general x9, matrix products, transform(): jnp.dot(forward, block, precision=lax.Precision.HIGHEST, preferred_elemen...  44.4 us
    cond x40, local copies, waits for them, and re-layouts  14.4 us
    dot_general x1, matrix products, per_device(): projected = jnp.dot(gated, out_weight, preferred_element_type=jnp.float32)  14.1 us
  transfers between devices with their start and end apart: 4, of which 3 were waited for; matrix products, arithmetic and copies ran while one was open for 4% of the time, Pallas kernels for 0%

commit v1 on v0

v1 whole, which is shorter than its diff:
```python
import numpy as np

import jax
import jax.numpy as jnp
import ml_dtypes
from jax import lax
from jax.experimental import pallas as pl
from jax.experimental.pallas import tpu as pltpu
from jax.sharding import PartitionSpec as P

GROUP_CH = 256
SPAN = 512
WIDTH = 512
NCTX = 8
OWN = WIDTH // NCTX
HALF = SPAN // 2
QUART = SPAN // 4
BF = jnp.bfloat16
F32 = jnp.float32
MESH = pl.DeviceIdType.MESH


def tables():
    freq = np.concatenate([np.arange(0, SPAN, 2), np.arange(1, SPAN, 2)])
    angle = np.pi * ((np.arange(SPAN)[:, None] * (2 * freq + 1)[None, :]) % (4 * SPAN)) / (2 * SPAN)
    forward = np.concatenate([np.cos(angle), -np.sin(angle)], axis=1)
    high = forward.astype(ml_dtypes.bfloat16)
    low = (forward - high.astype(np.float64)).astype(ml_dtypes.bfloat16)
    scale = ml_dtypes.bfloat16(1.0 / SPAN)
    return (
        np.stack([high, low]),
        np.stack([np.ascontiguousarray(high.T) * scale, np.ascontiguousarray(low.T) * scale]),
    )


def nt(lhs, rhs):
    return lax.dot_general(lhs, rhs, (((1,), (1,)), ((), ())), preferred_element_type=F32)


def mm(lhs, rhs):
    return jnp.dot(lhs, rhs, preferred_element_type=F32)


def kernel(
    lens, sw, skip, feat, filt, weight, fwd_hbm, inv_hbm,
    out,
    ext, halo, ftmp, fsend, frecv, sbf, ssend, srecv, qbuf, sbuf, fwd, inv, eye,
    spec_h, spec_x, spec_y, yhi, ylo, csend, crecv, gbuf, wbuf,
    xsend, xrecv, z1send, z1recv, z2send, z2recv, zxsend, zxrecv,
    s1send, s1recv, s2send, s2recv, keep,
    loc, wloc, hs, hr, fs, fr, ss, sr, ws, wr, cs, cr, gs, gr,
    xs, xr, z1s, z1r, z2s, z2r, zxs, zxr, s1s, s1r, s2s, s2r,
):
    c, g = lax.axis_index("ctx"), lax.axis_index("grp")
    z, xh, core = g // 4, (g // 2) % 2, g % 2
    partner = (c, g + 1 - 2 * core)
    across = (c, g + 2 - 4 * xh)
    up = (c, ((z + 1) % 4) * 4 + xh * 2 + core)
    down = (c, ((z + 3) % 4) * 4 + xh * 2 + core)

    def remote(src, dst, send, recv, device):
        return pltpu.make_async_remote_copy(
            src_ref=src, dst_ref=dst, send_sem=send, recv_sem=recv, device_id=device, device_id_type=MESH
        )

    sent = []

    def start(*args):
        copy = remote(*args)
        copy.start()
        sent.append(copy)

    def arrived(dst, recv):
        remote(dst, dst, hs.at[0], recv, partner).wait_recv()

    def rows64(ref, index):
        return ref.at[pl.ds(pl.multiple_of(index * OWN, OWN), OWN)]

    get_filt = pltpu.make_async_copy(filt, ftmp, loc.at[0])
    get_feat = pltpu.make_async_copy(feat, ext.at[:, pl.ds(16, SPAN)], loc.at[1])
    get_fwd = pltpu.make_async_copy(fwd_hbm, fwd, loc.at[2])
    get_inv = pltpu.make_async_copy(inv_hbm, inv, loc.at[3])
    get_filt.start()
    get_feat.start()
    get_fwd.start()
    get_inv.start()
    mine = pl.ds(pl.multiple_of(core * WIDTH, WIDTH), WIDTH)

    barrier = pltpu.get_barrier_semaphore()
    peers = [(lax.rem(c + k, NCTX), g) for k in range(1, NCTX)]
    for device in peers + [partner, across, up, down]:
        pl.semaphore_signal(barrier, inc=1, device_id=device, device_id_type=MESH)

    eye[...] = (
        lax.broadcasted_iota(jnp.int32, (HALF, HALF), 0) == lax.broadcasted_iota(jnp.int32, (HALF, HALF), 1)
    ).astype(F32).astype(BF)
    get_filt.wait()
    for part in range(WIDTH // GROUP_CH):
        length = lens[2 * g + part]
        cols = pl.ds(part * GROUP_CH, GROUP_CH)
        lag = c * SPAN + lax.broadcasted_iota(jnp.int32, (SPAN, GROUP_CH), 0)
        cut = jnp.where(lag < length, ftmp[:, cols].astype(F32), 0.0).astype(BF)
        fsend[cols, :] = nt(eye[...], cut).astype(BF)

    pl.semaphore_wait(barrier, len(peers) + 4)
    start(feat.at[:, pl.ds(SPAN - 16, 16)], halo, hs.at[0], hr.at[0], peers[0])
    for k, peer in enumerate(peers):
        start(rows64(fsend, peer[0]), rows64(frecv, c), fs.at[k], fr.at[c], peer)
    own_f = pltpu.make_async_copy(rows64(fsend, c), rows64(frecv, c), fr.at[c])
    own_f.start()

    get_feat.wait()

    def short(block):
        base = pl.multiple_of(block * 32, 32)
        here = pl.ds(base, 32)
        res = []
        for i in range(3):
            v = ext[i, pl.ds(base, 48), :].astype(F32)
            acc = sw[0, i : i + 1, :] * v[16:]
            acc = acc + sw[1, i : i + 1, :] * pltpu.roll(v, 1, 0)[16:]
            acc = acc + sw[2, i : i + 1, :] * pltpu.roll(v, 2, 0)[16:]
            res.append(acc)
        qbuf[here, :] = res[0]
        signal = res[1] * res[2]
        sbuf[here, :] = signal
        sbf[here, :] = signal.astype(BF)

    @pl.loop(1, SPAN // 32)
    def _(block):
        short(block)

    arrived(halo, hr.at[0])
    first = lax.broadcast_in_dim(c, (3, 16, WIDTH), ()) > 0
    ext[:, pl.ds(0, 16), :] = jnp.where(first, halo[...].astype(F32), 0.0).astype(BF)
    short(0)
    for part in range(2):
        cols = pl.ds(part * HALF, HALF)
        ssend[cols, :] = nt(eye[...], sbf[:, cols]).astype(BF)
    for k, peer in enumerate(peers):
        start(rows64(ssend, peer[0]), rows64(srecv, c), ss.at[k], sr.at[c], peer)
    own_s = pltpu.make_async_copy(rows64(ssend, c), rows64(srecv, c), sr.at[c])
    own_s.start()

    get_w = []
    for p in range(8):
        keep_cols = pl.ds(pl.multiple_of((2 * p + core) * WIDTH, WIDTH), WIDTH)
        give_cols = pl.ds(pl.multiple_of((2 * p + 1 - core) * WIDTH, WIDTH), WIDTH)
        copy = pltpu.make_async_copy(weight.at[:, keep_cols], wbuf.at[p, mine], wloc.at[p])
        copy.start()
        get_w.append(copy)
        start(weight.at[:, give_cols], wbuf.at[p, mine], ws.at[p], wr.at[p], partner)

    get_fwd.wait()

    def transform(block, spec):
        @pl.loop(0, 4)
        def _(n):
            cols = pl.ds(pl.multiple_of(n * HALF, HALF), HALF)
            spec[:, cols] = mm(block[...], fwd[0, :, cols]) + mm(block[...], fwd[1, :, cols])

    for k in range(NCTX):
        arrived(rows64(frecv, k), fr.at[k])
    transform(frecv, spec_h)
    for k in range(NCTX):
        arrived(rows64(srecv, k), sr.at[k])
    transform(srecv, spec_x)

    for lane in range(4):
        re, im = pl.ds(lane * 128, 128), pl.ds(SPAN + lane * 128, 128)

        @pl.loop(0, OWN // 8)
        def _(r, re=re, im=im, odd=lane >= 2):
            def at(spec, block, cols):
                return spec[pl.ds(pl.multiple_of(block * OWN + r * 8, 8), 8), cols]

            h_re = [at(spec_h, d, re) for d in range(NCTX)]
            h_im = [at(spec_h, d, im) for d in range(NCTX)]
            if odd:
                g_re = [h_re[0]] + [h_re[d] + h_im[d - 1] for d in range(1, NCTX)]
                g_im = [h_im[0]] + [h_im[d] - h_re[d - 1] for d in range(1, NCTX)]
            else:
                g_re = [h_re[0]] + [h_re[d] - h_im[d - 1] for d in range(1, NCTX)]
                g_im = [h_im[0]] + [h_im[d] + h_re[d - 1] for d in range(1, NCTX)]
            x_re = [at(spec_x, j, re) for j in range(NCTX)]
            x_im = [at(spec_x, j, im) for j in range(NCTX)]
            for i in range(NCTX):
                y_re = x_re[0] * g_re[i] - x_im[0] * g_im[i]
                y_im = x_re[0] * g_im[i] + x_im[0] * g_re[i]
                for j in range(1, i + 1):
                    y_re = y_re + x_re[j] * g_re[i - j] - x_im[j] * g_im[i - j]
                    y_im = y_im + x_re[j] * g_im[i - j] + x_im[j] * g_re[i - j]
                rows = pl.ds(pl.multiple_of(i * OWN + r * 8, 8), 8)
                spec_y[rows, re] = y_re
                spec_y[rows, im] = y_im

    @pl.loop(0, 16)
    def _(r):
        rows = pl.ds(pl.multiple_of(r * 32, 32), 32)
        value = spec_y[rows, :]
        high = value.astype(BF)
        yhi[rows, :] = high
        ylo[rows, :] = (value - high.astype(F32)).astype(BF)

    get_inv.wait()
    for h in range(2):
        cols = pl.ds(h * HALF, HALF)
        back = mm(yhi[...], inv[0, :, cols]) + mm(ylo[...], inv[0, :, cols]) + mm(yhi[...], inv[1, :, cols])
        csend[h] = back.astype(BF)
        for k, peer in enumerate(peers):
            start(
                rows64(csend.at[h], peer[0]), rows64(crecv.at[h], c), cs.at[h, k], cr.at[h, c], peer
            )
        pltpu.make_async_copy(rows64(csend.at[h], c), rows64(crecv.at[h], c), cr.at[h, c]).start()

    def gate(h):
        for k in range(NCTX):
            arrived(rows64(crecv.at[h], k), cr.at[h, k])
        rows = pl.ds(h * HALF, HALF)
        conv = nt(eye[...], crecv[h])
        gated = qbuf[rows, :] * (conv + skip[...] * sbuf[rows, :])
        gbuf[h, core] = gated.astype(BF)
        start(gbuf.at[h, core], gbuf.at[h, core], gs.at[h], gr.at[h], partner)

    def met(h):
        arrived(gbuf.at[h, 1 - core], gr.at[h])

    def project(h, dz, other):
        p = ((z + dz) % 4) * 2 + (xh if other == 0 else 1 - xh)
        return mm(gbuf[h, 0], wbuf[p, :WIDTH, :]) + mm(gbuf[h, 1], wbuf[p, WIDTH:, :])

    top, low = pl.ds(0, QUART), pl.ds(QUART, QUART)

    gate(0)
    gate(1)
    for p in range(8):
        get_w[p].wait()
        arrived(wbuf.at[p, pl.ds(pl.multiple_of((1 - core) * WIDTH, WIDTH), WIDTH)], wr.at[p])
    met(0)
    for dz in (2, 1, 3, 0):
        xsend[dz] = project(0, dz, 1).astype(BF)
        start(xsend.at[dz], xrecv.at[dz], xs.at[dz], xr.at[dz], across)
    met(1)
    for o in range(2):
        z1send[o] = project(1, 2, o).astype(BF)
        start(z1send.at[o, top], z1recv.at[0, o], z1s.at[0, o], z1r.at[0, o], up)
        start(z1send.at[o, low], z1recv.at[1, o], z1s.at[1, o], z1r.at[1, o], down)
    for d, dz, rows, device in ((0, 1, top, up), (1, 3, low, down)):
        for o in range(2):
            z2send[d, o] = project(1, dz, o).astype(BF)
            arrived(z1recv.at[d, o], z1r.at[d, o])
            z2send[d, o, rows] = (z2send[d, o, rows].astype(F32) + z1recv[d, o].astype(F32)).astype(BF)
            start(z2send.at[d, o], z2recv.at[d, o], z2s.at[d, o], z2r.at[d, o], device)

    def summed(dz):
        keep[...] = project(0, dz, 0)
        arrived(xrecv.at[dz], xr.at[dz])
        keep[...] += xrecv[dz].astype(F32)

    summed(2)
    s1send[...] = keep[...].astype(BF)
    start(s1send.at[top], s1recv.at[0], s1s.at[0], s1r.at[0], up)
    start(s1send.at[low], s1recv.at[1], s1s.at[1], s1r.at[1], down)
    for d, dz, rows, device in ((0, 1, top, up), (1, 3, low, down)):
        summed(dz)
        arrived(s1recv.at[d], s1r.at[d])
        keep[rows, :] += s1recv[d].astype(F32)
        s2send[d] = keep[...].astype(BF)
        start(s2send.at[d], s2recv.at[d], s2s.at[d], s2r.at[d], device)

    def gathered(o):
        keep[...] = project(1, 0, o)
        for d in range(2):
            arrived(z2recv.at[d, o], z2r.at[d, o])
        keep[...] += z2recv[0, o].astype(F32) + z2recv[1, o].astype(F32)

    gathered(1)
    zxsend[...] = keep[...].astype(BF)
    start(zxsend, zxrecv, zxs.at[0], zxr.at[0], across)
    summed(0)
    for d in range(2):
        arrived(s2recv.at[d], s2r.at[d])
    out[pl.ds(0, HALF), :] = (keep[...] + s2recv[0].astype(F32) + s2recv[1].astype(F32)).astype(BF)
    gathered(0)
    arrived(zxrecv, zxr.at[0])
    out[pl.ds(HALF, HALF), :] = (keep[...] + zxrecv[...].astype(F32)).astype(BF)
    for copy in sent:
        copy.wait_send()


def per_device(features, short_weight, long_filter, lengths, skip_gain, out_weight):
    forward, inverse = tables()
    dma = pltpu.SemaphoreType.DMA
    vm = pltpu.VMEM
    block = (HALF, WIDTH)
    scratch = [
        vm((3, 16 + SPAN, WIDTH), BF), vm((3, 16, WIDTH), BF),
        vm((SPAN, WIDTH), BF), vm((WIDTH, SPAN), BF), vm((WIDTH, SPAN), BF),
        vm((SPAN, WIDTH), BF), vm((WIDTH, SPAN), BF), vm((WIDTH, SPAN), BF),
        vm((SPAN, WIDTH), F32), vm((SPAN, WIDTH), F32),
        vm((2, SPAN, 2 * SPAN), BF), vm((2, 2 * SPAN, SPAN), BF), vm((HALF, HALF), BF),
        vm((WIDTH, 2 * SPAN), F32), vm((WIDTH, 2 * SPAN), F32), vm((WIDTH, 2 * SPAN), F32),
        vm((WIDTH, 2 * SPAN), BF), vm((WIDTH, 2 * SPAN), BF),
        vm((2, WIDTH, HALF), BF), vm((2, WIDTH, HALF), BF),
        vm((2, 2) + block, BF), vm((8, 2 * WIDTH, WIDTH), BF),
        vm((4,) + block, BF), vm((4,) + block, BF),
        vm((2,) + block, BF), vm((2, 2, QUART, WIDTH), BF),
        vm((2, 2) + block, BF), vm((2, 2) + block, BF),
        vm(block, BF), vm(block, BF),
        vm(block, BF), vm((2, QUART, WIDTH), BF),
        vm((2,) + block, BF), vm((2,) + block, BF), vm(block, F32),
        dma((4,)), dma((8,)), dma((1,)), dma((1,)),
        dma((7,)), dma((8,)), dma((7,)), dma((8,)), dma((8,)), dma((8,)),
        dma((2, 7)), dma((2, 8)), dma((2,)), dma((2,)),
        dma((4,)), dma((4,)), dma((2, 2)), dma((2, 2)), dma((2, 2)), dma((2, 2)),
        dma((1,)), dma((1,)), dma((2,)), dma((2,)), dma((2,)), dma((2,)),
    ]
    hbm = pl.BlockSpec(memory_space=pl.ANY)
    near = pl.BlockSpec(memory_space=pltpu.VMEM)
    return pl.pallas_call(
        kernel,
        out_shape=jax.ShapeDtypeStruct((SPAN, WIDTH), BF),
        in_specs=[pl.BlockSpec(memory_space=pltpu.SMEM), near, near, hbm, hbm, hbm, hbm, hbm],
        out_specs=near,
        scratch_shapes=scratch,
        name="hyena",
        compiler_params=pltpu.CompilerParams(
            collective_id=0, has_side_effects=True, vmem_limit_bytes=56 * 2**20
        ),
    )(
        lengths, short_weight, skip_gain.reshape(1, WIDTH), features, long_filter, out_weight,
        jnp.asarray(forward), jnp.asarray(inverse),
    )


def solution(mesh):
    return jax.shard_map(
        per_device,
        mesh=mesh,
        in_specs=(
            P(None, "ctx", "grp"),
            P(None, None, "grp"),
            P("ctx", "grp"),
            P(),
            P("grp"),
            P("grp", None),
        ),
        out_specs=P("ctx", "grp"),
        check_vma=False,
    )
```

time: 679 us -> 73.8 us (0.11); the launches traced: 669 us -> 73.6 us
  waiting for transfers between devices: 376 us -> 0 us
  matrix products: 189 us -> 0 us
  Pallas kernels: 0 us -> 71.7 us
  local copies, waits for them, and re-layouts: 42.7 us -> 1.87 us
  other arithmetic: 37 us -> 0 us
  between operations: 18.8 us -> 0.01 us
    reduce_scatter x2 -> x0, waiting for transfers between devices: 318 us -> none  [the longest x1 169 us: per_device(): lax.psum_scatter(buffer[:nctx * span], 'ctx', scatter_dimension=0, tiled=...]
    dot_general x18 -> x0, matrix products: 189 us -> none  [the longest x8 130 us: product_back(): jnp.dot(inverse, stacked, precision=lax.Precision.HIGHEST, preferred_elem...]
    pallas_call x0 -> x1, Pallas kernels: none -> 71.7 us  [per_device(): pl.pallas_call(kernel, out_shape=jax.ShapeDtypeStruct((SPAN, WIDTH), BF),...]
    all_gather x1 -> x0, waiting for transfers between devices: 57.2 us -> none  [per_device(): all_taps = lax.all_gather(long_filter, 'ctx', axis=0, tiled=True)]
    cond x41 -> x0, local copies, waits for them, and re-layouts: 16 us -> none
    add x7 -> x0, local copies, waits for them, and re-layouts: 11.2 us -> none  [per_device(): partials.append(window[:span] + tail)]
    mul x1 -> x0, other arithmetic: 10.8 us -> none  [tables(): -weight * jnp.sin(angle_back)]
    add x9 -> x0, other arithmetic: 9.84 us -> none  [the longest x1 8.89 us: per_device(): partials.append(window[:span] + tail)]
  transfers between devices with their start and end apart: 4 -> 0, of which waited for: 3 -> 0; matrix products, arithmetic and copies ran while one was open for 4% -> 0% of each run, Pallas kernels for 0% -> 0%
where the time goes in v1:
time: 73.8 us; the launch traced here: 73.6 us
  Pallas kernels  71.7 us (97%)
  local copies, waits for them, and re-layouts  1.87 us (3%)
    pallas_call x1, Pallas kernels, per_device(): pl.pallas_call(kernel, out_shape=jax.ShapeDtypeStruct((SPAN, WIDTH), BF),...  71.7 us
    unnamed x1, local copies, waits for them, and re-layouts  1.87 us

profile of v1, /device:TPU:0, one launch (start us, length us, event | category | flops | bytes accessed | tf_op | source)
XLA Modules:
  0.0 73.6 jit_solution(16252419030718133718)
XLA Ops:
  0.0 71.7 %hyena.1 = bf16[512,512]{1,0:T(8,128)(2,1)} custom-call(s32[32]{0:T(128)} %lens.1, f32[3,3,512]{2,1,0:T(4,128)} %sw.1, f32[1,512]{1,0:T(1,128)} %bitcast.1, bf16[3,512,512]{2,1,0:T(8,128)(2,1)} %feat.1, bf16[512,512]{1,0:T(8,128)(2,1)} %filt.1, bf16[512,8192]{1,0:T(8,128)(2,1)} %weight.1, bf16[2,512,1024]{2,1,0:T(8,128)(2,1)} %constant.4.clone.fwd_hbm, ...), custom_call_target="tpu_custom_call" | custom-call | tf_op jit(solution)/shard_map/hyena/pallas_call | solution.py:320
  71.8 1.9 %copy.10 = bf16[512,512]{1,0:T(8,128)(2,1)} copy(bf16[512,512]{1,0:T(8,128)(2,1)} %hyena.1) | data formatting | bytes 1048576

commit v2 on v1

--- a/solution.py
+++ b/solution.py
@@ -13,6 +13,7 @@
 WIDTH = 512
 NCTX = 8
 OWN = WIDTH // NCTX
+BATCH = OWN // 2
 HALF = SPAN // 2
 QUART = SPAN // 4
 BF = jnp.bfloat16
@@ -44,7 +45,7 @@
 def kernel(
     lens, sw, skip, feat, filt, weight, fwd_hbm, inv_hbm,
     out,
-    ext, halo, ftmp, fsend, frecv, sbf, ssend, srecv, qbuf, sbuf, fwd, inv, eye,
+    ext, edge, halo, ftmp, fsend, frecv, sbf, ssend, srecv, qbuf, sbuf, fwd, inv, eye,
     spec_h, spec_x, spec_y, yhi, ylo, csend, crecv, gbuf, wbuf,
     xsend, xrecv, z1send, z1recv, z2send, z2recv, zxsend, zxrecv,
     s1send, s1recv, s2send, s2recv, keep,
@@ -76,6 +77,9 @@
     def rows64(ref, index):
         return ref.at[pl.ds(pl.multiple_of(index * OWN, OWN), OWN)]
 
+    def rows32(ref, index):
+        return ref.at[pl.ds(pl.multiple_of(index * BATCH, BATCH), BATCH)]
+
     get_filt = pltpu.make_async_copy(filt, ftmp, loc.at[0])
     get_feat = pltpu.make_async_copy(feat, ext.at[:, pl.ds(16, SPAN)], loc.at[1])
     get_fwd = pltpu.make_async_copy(fwd_hbm, fwd, loc.at[2])
@@ -102,14 +106,21 @@
         cut = jnp.where(lag < length, ftmp[:, cols].astype(F32), 0.0).astype(BF)
         fsend[cols, :] = nt(eye[...], cut).astype(BF)
 
+    get_feat.wait()
+    row = lax.broadcasted_iota(jnp.int32, (16, WIDTH), 0)
+    packed = jnp.zeros((16, WIDTH), F32)
+    for i in range(3):
+        last = pltpu.roll(ext[i, pl.ds(SPAN, 16), :].astype(F32), 2 + 2 * i, 0)
+        packed = jnp.where(row // 2 == i, last, packed)
+    edge[...] = packed.astype(BF)
+
     pl.semaphore_wait(barrier, len(peers) + 4)
-    start(feat.at[:, pl.ds(SPAN - 16, 16)], halo, hs.at[0], hr.at[0], peers[0])
+    start(edge, halo, hs.at[0], hr.at[0], peers[0])
     for k, peer in enumerate(peers):
         start(rows64(fsend, peer[0]), rows64(frecv, c), fs.at[k], fr.at[c], peer)
     own_f = pltpu.make_async_copy(rows64(fsend, c), rows64(frecv, c), fr.at[c])
     own_f.start()
 
-    get_feat.wait()
 
     def short(block):
         base = pl.multiple_of(block * 32, 32)
@@ -131,16 +142,17 @@
         short(block)
 
     arrived(halo, hr.at[0])
-    first = lax.broadcast_in_dim(c, (3, 16, WIDTH), ()) > 0
-    ext[:, pl.ds(0, 16), :] = jnp.where(first, halo[...].astype(F32), 0.0).astype(BF)
+    before = jnp.where(lax.broadcast_in_dim(c, (16, WIDTH), ()) > 0, halo[...].astype(F32), 0.0)
+    for i in range(3):
+        ext[i, pl.ds(0, 16), :] = pltpu.roll(before, 14 - 2 * i, 0).astype(BF)
     short(0)
     for part in range(2):
         cols = pl.ds(part * HALF, HALF)
         ssend[cols, :] = nt(eye[...], sbf[:, cols]).astype(BF)
-    for k, peer in enumerate(peers):
-        start(rows64(ssend, peer[0]), rows64(srecv, c), ss.at[k], sr.at[c], peer)
-    own_s = pltpu.make_async_copy(rows64(ssend, c), rows64(srecv, c), sr.at[c])
-    own_s.start()
+    for b in range(2):
+        for k, peer in enumerate(peers):
+            start(rows32(ssend, 2 * peer[0] + b), rows32(srecv.at[b], c), ss.at[b, k], sr.at[b, c], peer)
+        pltpu.make_async_copy(rows32(ssend, 2 * c + b), rows32(srecv.at[b], c), sr.at[b, c]).start()
 
     get_w = []
     for p in range(8):
@@ -162,60 +174,70 @@
     for k in range(NCTX):
         arrived(rows64(frecv, k), fr.at[k])
     transform(frecv, spec_h)
-    for k in range(NCTX):
-        arrived(rows64(srecv, k), sr.at[k])
-    transform(srecv, spec_x)
-
-    for lane in range(4):
-        re, im = pl.ds(lane * 128, 128), pl.ds(SPAN + lane * 128, 128)
-
-        @pl.loop(0, OWN // 8)
-        def _(r, re=re, im=im, odd=lane >= 2):
-            def at(spec, block, cols):
-                return spec[pl.ds(pl.multiple_of(block * OWN + r * 8, 8), 8), cols]
-
-            h_re = [at(spec_h, d, re) for d in range(NCTX)]
-            h_im = [at(spec_h, d, im) for d in range(NCTX)]
-            if odd:
-                g_re = [h_re[0]] + [h_re[d] + h_im[d - 1] for d in range(1, NCTX)]
-                g_im = [h_im[0]] + [h_im[d] - h_re[d - 1] for d in range(1, NCTX)]
-            else:
-                g_re = [h_re[0]] + [h_re[d] - h_im[d - 1] for d in range(1, NCTX)]
-                g_im = [h_im[0]] + [h_im[d] + h_re[d - 1] for d in range(1, NCTX)]
-            x_re = [at(spec_x, j, re) for j in range(NCTX)]
-            x_im = [at(spec_x, j, im) for j in range(NCTX)]
-            for i in range(NCTX):
-                y_re = x_re[0] * g_re[i] - x_im[0] * g_im[i]
-                y_im = x_re[0] * g_im[i] + x_im[0] * g_re[i]
-                for j in range(1, i + 1):
-                    y_re = y_re + x_re[j] * g_re[i - j] - x_im[j] * g_im[i - j]
-                    y_im = y_im + x_re[j] * g_im[i - j] + x_im[j] * g_re[i - j]
-                rows = pl.ds(pl.multiple_of(i * OWN + r * 8, 8), 8)
-                spec_y[rows, re] = y_re
-                spec_y[rows, im] = y_im
-
-    @pl.loop(0, 16)
-    def _(r):
-        rows = pl.ds(pl.multiple_of(r * 32, 32), 32)
-        value = spec_y[rows, :]
-        high = value.astype(BF)
-        yhi[rows, :] = high
-        ylo[rows, :] = (value - high.astype(F32)).astype(BF)
-
-    get_inv.wait()
-    for h in range(2):
+
+    def products(b):
+        for lane in range(4):
+            re, im = pl.ds(lane * 128, 128), pl.ds(SPAN + lane * 128, 128)
+
+            @pl.loop(0, BATCH // 8)
+            def _(r, re=re, im=im, odd=lane >= 2):
+                def rows(block, size, base):
+                    return pl.ds(pl.multiple_of(block * size + base + r * 8, 8), 8)
+
+                h_re = [spec_h[rows(d, OWN, b * BATCH), re] for d in range(NCTX)]
+                h_im = [spec_h[rows(d, OWN, b * BATCH), im] for d in range(NCTX)]
+                if odd:
+                    g_re = [h_re[0]] + [h_re[d] + h_im[d - 1] for d in range(1, NCTX)]
+                    g_im = [h_im[0]] + [h_im[d] - h_re[d - 1] for d in range(1, NCTX)]
+                else:
+                    g_re = [h_re[0]] + [h_re[d] - h_im[d - 1] for d in range(1, NCTX)]
+                    g_im = [h_im[0]] + [h_im[d] + h_re[d - 1] for d in range(1, NCTX)]
+                x_re = [spec_x[b, rows(j, BATCH, 0), re] for j in range(NCTX)]
+                x_im = [spec_x[b, rows(j, BATCH, 0), im] for j in range(NCTX)]
+                for i in range(NCTX):
+                    y_re = x_re[0] * g_re[i] - x_im[0] * g_im[i]
+                    y_im = x_re[0] * g_im[i] + x_im[0] * g_re[i]
+                    for j in range(1, i + 1):
+                        y_re = y_re + x_re[j] * g_re[i - j] - x_im[j] * g_im[i - j]
+                        y_im = y_im + x_re[j] * g_im[i - j] + x_im[j] * g_re[i - j]
+                    spec_y[b, rows(i, BATCH, 0), re] = y_re
+                    spec_y[b, rows(i, BATCH, 0), im] = y_im
+
+        @pl.loop(0, 8)
+        def _(r):
+            rows = pl.ds(pl.multiple_of(r * 32, 32), 32)
+            value = spec_y[b, rows, :]
+            high = value.astype(BF)
+            yhi[b, rows, :] = high
+            ylo[b, rows, :] = (value - high.astype(F32)).astype(BF)
+
+    def inverse(b, h):
         cols = pl.ds(h * HALF, HALF)
-        back = mm(yhi[...], inv[0, :, cols]) + mm(ylo[...], inv[0, :, cols]) + mm(yhi[...], inv[1, :, cols])
-        csend[h] = back.astype(BF)
+        back = mm(yhi[b], inv[0, :, cols]) + mm(ylo[b], inv[0, :, cols]) + mm(yhi[b], inv[1, :, cols])
+        csend[h, b] = back.astype(BF)
         for k, peer in enumerate(peers):
             start(
-                rows64(csend.at[h], peer[0]), rows64(crecv.at[h], c), cs.at[h, k], cr.at[h, c], peer
+                rows32(csend.at[h, b], peer[0]), rows32(crecv.at[h], 2 * c + b),
+                cs.at[h, b, k], cr.at[h, b, c], peer,
             )
-        pltpu.make_async_copy(rows64(csend.at[h], c), rows64(crecv.at[h], c), cr.at[h, c]).start()
+        pltpu.make_async_copy(
+            rows32(csend.at[h, b], c), rows32(crecv.at[h], 2 * c + b), cr.at[h, b, c]
+        ).start()
+
+    get_inv.wait()
+    for b in range(2):
+        for k in range(NCTX):
+            arrived(rows32(srecv.at[b], k), sr.at[b, k])
+        transform(srecv.at[b], spec_x.at[b])
+        products(b)
+        inverse(b, 0)
+    for b in range(2):
+        inverse(b, 1)
 
     def gate(h):
-        for k in range(NCTX):
-            arrived(rows64(crecv.at[h], k), cr.at[h, k])
+        for b in range(2):
+            for k in range(NCTX):
+                arrived(rows32(crecv.at[h], 2 * k + b), cr.at[h, b, k])
         rows = pl.ds(h * HALF, HALF)
         conv = nt(eye[...], crecv[h])
         gated = qbuf[rows, :] * (conv + skip[...] * sbuf[rows, :])
@@ -232,7 +254,6 @@
     top, low = pl.ds(0, QUART), pl.ds(QUART, QUART)
 
     gate(0)
-    gate(1)
     for p in range(8):
         get_w[p].wait()
         arrived(wbuf.at[p, pl.ds(pl.multiple_of((1 - core) * WIDTH, WIDTH), WIDTH)], wr.at[p])
@@ -240,16 +261,19 @@
     for dz in (2, 1, 3, 0):
         xsend[dz] = project(0, dz, 1).astype(BF)
         start(xsend.at[dz], xrecv.at[dz], xs.at[dz], xr.at[dz], across)
+    gate(1)
     met(1)
-    for o in range(2):
+    for o in (1, 0):
         z1send[o] = project(1, 2, o).astype(BF)
         start(z1send.at[o, top], z1recv.at[0, o], z1s.at[0, o], z1r.at[0, o], up)
         start(z1send.at[o, low], z1recv.at[1, o], z1s.at[1, o], z1r.at[1, o], down)
-    for d, dz, rows, device in ((0, 1, top, up), (1, 3, low, down)):
-        for o in range(2):
-            z2send[d, o] = project(1, dz, o).astype(BF)
+
+    def second(o):
+        for d, dz, rows, device in ((0, 1, top, up), (1, 3, low, down)):
+            keep[...] = project(1, dz, o)
             arrived(z1recv.at[d, o], z1r.at[d, o])
-            z2send[d, o, rows] = (z2send[d, o, rows].astype(F32) + z1recv[d, o].astype(F32)).astype(BF)
+            keep[rows, :] += z1recv[d, o].astype(F32)
+            z2send[d, o] = keep[...].astype(BF)
             start(z2send.at[d, o], z2recv.at[d, o], z2s.at[d, o], z2r.at[d, o], device)
 
     def summed(dz):
@@ -257,11 +281,7 @@
         arrived(xrecv.at[dz], xr.at[dz])
         keep[...] += xrecv[dz].astype(F32)
 
-    summed(2)
-    s1send[...] = keep[...].astype(BF)
-    start(s1send.at[top], s1recv.at[0], s1s.at[0], s1r.at[0], up)
-    start(s1send.at[low], s1recv.at[1], s1s.at[1], s1r.at[1], down)
-    for d, dz, rows, device in ((0, 1, top, up), (1, 3, low, down)):
+    def forward(d, dz, rows, device):
         summed(dz)
         arrived(s1recv.at[d], s1r.at[d])
         keep[rows, :] += s1recv[d].astype(F32)
@@ -274,9 +294,17 @@
             arrived(z2recv.at[d, o], z2r.at[d, o])
         keep[...] += z2recv[0, o].astype(F32) + z2recv[1, o].astype(F32)
 
+    second(1)
+    summed(2)
+    s1send[...] = keep[...].astype(BF)
+    start(s1send.at[top], s1recv.at[0], s1s.at[0], s1r.at[0], up)
+    start(s1send.at[low], s1recv.at[1], s1s.at[1], s1r.at[1], down)
+    second(0)
+    forward(0, 1, top, up)
     gathered(1)
     zxsend[...] = keep[...].astype(BF)
     start(zxsend, zxrecv, zxs.at[0], zxr.at[0], across)
+    forward(1, 3, low, down)
     summed(0)
     for d in range(2):
         arrived(s2recv.at[d], s2r.at[d])
@@ -294,14 +322,14 @@
     vm = pltpu.VMEM
     block = (HALF, WIDTH)
     scratch = [
-        vm((3, 16 + SPAN, WIDTH), BF), vm((3, 16, WIDTH), BF),
+        vm((3, 16 + SPAN, WIDTH), BF), vm((16, WIDTH), BF), vm((16, WIDTH), BF),
         vm((SPAN, WIDTH), BF), vm((WIDTH, SPAN), BF), vm((WIDTH, SPAN), BF),
-        vm((SPAN, WIDTH), BF), vm((WIDTH, SPAN), BF), vm((WIDTH, SPAN), BF),
+        vm((SPAN, WIDTH), BF), vm((WIDTH, SPAN), BF), vm((2, WIDTH // 2, SPAN), BF),
         vm((SPAN, WIDTH), F32), vm((SPAN, WIDTH), F32),
         vm((2, SPAN, 2 * SPAN), BF), vm((2, 2 * SPAN, SPAN), BF), vm((HALF, HALF), BF),
-        vm((WIDTH, 2 * SPAN), F32), vm((WIDTH, 2 * SPAN), F32), vm((WIDTH, 2 * SPAN), F32),
-        vm((WIDTH, 2 * SPAN), BF), vm((WIDTH, 2 * SPAN), BF),
-        vm((2, WIDTH, HALF), BF), vm((2, WIDTH, HALF), BF),
+        vm((WIDTH, 2 * SPAN), F32), vm((2, WIDTH // 2, 2 * SPAN), F32), vm((2, WIDTH // 2, 2 * SPAN), F32),
+        vm((2, WIDTH // 2, 2 * SPAN), BF), vm((2, WIDTH // 2, 2 * SPAN), BF),
+        vm((2, 2, WIDTH // 2, HALF), BF), vm((2, WIDTH, HALF), BF),
         vm((2, 2) + block, BF), vm((8, 2 * WIDTH, WIDTH), BF),
         vm((4,) + block, BF), vm((4,) + block, BF),
         vm((2,) + block, BF), vm((2, 2, QUART, WIDTH), BF),
@@ -310,8 +338,8 @@
         vm(block, BF), vm((2, QUART, WIDTH), BF),
         vm((2,) + block, BF), vm((2,) + block, BF), vm(block, F32),
         dma((4,)), dma((8,)), dma((1,)), dma((1,)),
-        dma((7,)), dma((8,)), dma((7,)), dma((8,)), dma((8,)), dma((8,)),
-        dma((2, 7)), dma((2, 8)), dma((2,)), dma((2,)),
+        dma((7,)), dma((8,)), dma((2, 7)), dma((2, 8)), dma((8,)), dma((8,)),
+        dma((2, 2, 7)), dma((2, 2, 8)), dma((2,)), dma((2,)),
         dma((4,)), dma((4,)), dma((2, 2)), dma((2, 2)), dma((2, 2)), dma((2, 2)),
         dma((1,)), dma((1,)), dma((2,)), dma((2,)), dma((2,)), dma((2,)),
     ]

time: 73.8 us -> 67.7 us (0.917)
  Pallas kernels: 71.7 us -> 65.6 us
    pallas_call x1, Pallas kernels: 71.7 us -> 65.6 us  [per_device(): pl.pallas_call(kernel, out_shape=jax.ShapeDtypeStruct((SPAN, WIDTH), BF),...]
where the time goes in v2:
time: 67.7 us; the launch traced here: 67.5 us
  Pallas kernels  65.6 us (97%)
  local copies, waits for them, and re-layouts  1.87 us (3%)
    pallas_call x1, Pallas kernels, per_device(): pl.pallas_call(kernel, out_shape=jax.ShapeDtypeStruct((SPAN, WIDTH), BF),...  65.6 us
    unnamed x1, local copies, waits for them, and re-layouts  1.87 us

profile of v2, /device:TPU:0, one launch (start us, length us, event | category | flops | bytes accessed | tf_op | source)
XLA Modules:
  0.0 67.5 jit_solution(12148763475751270881)
XLA Ops:
  0.0 65.6 %hyena.1 = bf16[512,512]{1,0:T(8,128)(2,1)} custom-call(s32[32]{0:T(128)} %lens.1, f32[3,3,512]{2,1,0:T(4,128)} %sw.1, f32[1,512]{1,0:T(1,128)} %bitcast.1, bf16[3,512,512]{2,1,0:T(8,128)(2,1)} %feat.1, bf16[512,512]{1,0:T(8,128)(2,1)} %filt.1, bf16[512,8192]{1,0:T(8,128)(2,1)} %weight.1, bf16[2,512,1024]{2,1,0:T(8,128)(2,1)} %constant.4.clone.fwd_hbm, ...), custom_call_target="tpu_custom_call" | custom-call | tf_op jit(solution)/shard_map/hyena/pallas_call | solution.py:348
  65.6 1.9 %copy.10 = bf16[512,512]{1,0:T(8,128)(2,1)} copy(bf16[512,512]{1,0:T(8,128)(2,1)} %hyena.1) | data formatting | bytes 1048576

commit v3 on v2

v3 whole, which is shorter than its diff:
```python
import numpy as np

import jax
import jax.numpy as jnp
import ml_dtypes
from jax import lax
from jax.experimental import pallas as pl
from jax.experimental.pallas import tpu as pltpu
from jax.sharding import PartitionSpec as P

GROUP_CH = 256
SPAN = 512
WIDTH = 512
NCTX = 8
OWN = WIDTH // NCTX
BATCHES = ((0, 32), (32, 32))
HALF = SPAN // 2
CHUNKS = ((0, 128), (128, 128), (256, 256))
EARLY = 384
BF = jnp.bfloat16
F32 = jnp.float32
MESH = pl.DeviceIdType.MESH


def tables():
    freq = np.concatenate([np.arange(0, SPAN, 2), np.arange(1, SPAN, 2)])
    angle = np.pi * ((np.arange(SPAN)[:, None] * (2 * freq + 1)[None, :]) % (4 * SPAN)) / (2 * SPAN)
    forward = np.concatenate([np.cos(angle), -np.sin(angle)], axis=1)
    high = forward.astype(ml_dtypes.bfloat16)
    low = (forward - high.astype(np.float64)).astype(ml_dtypes.bfloat16)
    scale = ml_dtypes.bfloat16(1.0 / SPAN)
    return (
        np.stack([high, low]),
        np.stack([np.ascontiguousarray(high.T) * scale, np.ascontiguousarray(low.T) * scale]),
    )


def nt(lhs, rhs):
    return lax.dot_general(lhs, rhs, (((1,), (1,)), ((), ())), preferred_element_type=F32)


def mm(lhs, rhs):
    return jnp.dot(lhs, rhs, preferred_element_type=F32)


def kernel(
    lens, sw, skip, feat, filt, weight, fwd_hbm, inv_hbm,
    out,
    ext, edge, halo, ftmp, fsend, frecv, sbf, ssend, srecv, qbuf, sbuf, fwd, inv, eye,
    spec_h, spec_x, spec_y, yhi, ylo, csend0, csend1, csend2, crecv0, crecv1, crecv2, gbuf, wbuf,
    za1, za1r, za2, za2r, zax, zaxr, zb1, zb1r, zb2, zb2r, zbx, zbxr,
    xa, xar, xa1, xa1r, xa2, xa2r, xb, xbr, xb1, xb1r, xb2, xb2r, keep_a, keep_b, keep_c, keep_d,
    loc, wloc, hs, hr, fs, fr, ss, sr, ws, wr, cs, cr, gs, gr,
    xs, xr, z1s, z1r, z2s, z2r, zxs, zxr, s1s, s1r, s2s, s2r,
):
    c, g = lax.axis_index("ctx"), lax.axis_index("grp")
    z, xh, core = g // 4, (g // 2) % 2, g % 2
    partner = (c, g + 1 - 2 * core)
    across = (c, g + 2 - 4 * xh)
    up = (c, ((z + 1) % 4) * 4 + xh * 2 + core)
    down = (c, ((z + 3) % 4) * 4 + xh * 2 + core)

    def remote(src, dst, send, recv, device):
        return pltpu.make_async_remote_copy(
            src_ref=src, dst_ref=dst, send_sem=send, recv_sem=recv, device_id=device, device_id_type=MESH
        )

    sent = []

    def start(*args):
        copy = remote(*args)
        copy.start()
        sent.append(copy)
        return copy

    def arrived(dst, recv):
        remote(dst, dst, hs.at[0], recv, partner).wait_recv()

    def rows64(ref, index):
        return ref.at[pl.ds(pl.multiple_of(index * OWN, OWN), OWN)]

    def rows16(ref, base, size):
        return ref.at[pl.ds(pl.multiple_of(base, 16), size)]

    get_filt = pltpu.make_async_copy(filt, ftmp, loc.at[0])
    get_feat = pltpu.make_async_copy(feat, ext.at[:, pl.ds(16, SPAN)], loc.at[1])
    get_fwd = pltpu.make_async_copy(fwd_hbm, fwd, loc.at[2])
    get_inv = pltpu.make_async_copy(inv_hbm, inv, loc.at[3])
    get_filt.start()
    get_feat.start()
    get_fwd.start()
    get_inv.start()
    mine = pl.ds(pl.multiple_of(core * WIDTH, WIDTH), WIDTH)

    barrier = pltpu.get_barrier_semaphore()
    peers = [(lax.rem(c + k, NCTX), g) for k in range(1, NCTX)]
    for device in peers + [partner, across, up, down]:
        pl.semaphore_signal(barrier, inc=1, device_id=device, device_id_type=MESH)

    eye[...] = (
        lax.broadcasted_iota(jnp.int32, (HALF, HALF), 0) == lax.broadcasted_iota(jnp.int32, (HALF, HALF), 1)
    ).astype(F32).astype(BF)
    get_filt.wait()
    for part in range(WIDTH // GROUP_CH):
        length = lens[2 * g + part]
        cols = pl.ds(part * GROUP_CH, GROUP_CH)
        lag = c * SPAN + lax.broadcasted_iota(jnp.int32, (SPAN, GROUP_CH), 0)
        cut = jnp.where(lag < length, ftmp[:, cols].astype(F32), 0.0).astype(BF)
        fsend[cols, :] = nt(eye[...], cut).astype(BF)

    get_feat.wait()
    row = lax.broadcasted_iota(jnp.int32, (16, WIDTH), 0)
    packed = jnp.zeros((16, WIDTH), F32)
    for i in range(3):
        last = pltpu.roll(ext[i, pl.ds(SPAN, 16), :].astype(F32), 2 + 2 * i, 0)
        packed = jnp.where(row // 2 == i, last, packed)
    edge[...] = packed.astype(BF)

    pl.semaphore_wait(barrier, len(peers) + 4)
    start(edge, halo, hs.at[0], hr.at[0], peers[0])
    for k, peer in enumerate(peers):
        start(rows64(fsend, peer[0]), rows64(frecv, c), fs.at[k], fr.at[c], peer)
    own_f = pltpu.make_async_copy(rows64(fsend, c), rows64(frecv, c), fr.at[c])
    own_f.start()


    def short(block):
        base = pl.multiple_of(block * 32, 32)
        here = pl.ds(base, 32)
        res = []
        for i in range(3):
            v = ext[i, pl.ds(base, 48), :].astype(F32)
            acc = sw[0, i : i + 1, :] * v[16:]
            acc = acc + sw[1, i : i + 1, :] * pltpu.roll(v, 1, 0)[16:]
            acc = acc + sw[2, i : i + 1, :] * pltpu.roll(v, 2, 0)[16:]
            res.append(acc)
        qbuf[here, :] = res[0]
        signal = res[1] * res[2]
        sbuf[here, :] = signal
        sbf[here, :] = signal.astype(BF)

    @pl.loop(1, SPAN // 32)
    def _(block):
        short(block)

    arrived(halo, hr.at[0])
    before = jnp.where(lax.broadcast_in_dim(c, (16, WIDTH), ()) > 0, halo[...].astype(F32), 0.0)
    for i in range(3):
        ext[i, pl.ds(0, 16), :] = pltpu.roll(before, 14 - 2 * i, 0).astype(BF)
    short(0)
    for part in range(2):
        cols = pl.ds(part * HALF, HALF)
        ssend[cols, :] = nt(eye[...], sbf[:, cols]).astype(BF)
    def send_signal(b):
        off, size = BATCHES[b]
        for k, peer in enumerate(peers):
            start(
                rows16(ssend, peer[0] * OWN + off, size), rows16(srecv, NCTX * off + c * size, size),
                ss.at[b, k], sr.at[b, c], peer,
            )
        pltpu.make_async_copy(
            rows16(ssend, c * OWN + off, size), rows16(srecv, NCTX * off + c * size, size), sr.at[b, c]
        ).start()

    send_signal(0)

    get_w = []
    for p in range(8):
        keep_cols = pl.ds(pl.multiple_of((2 * p + core) * WIDTH, WIDTH), WIDTH)
        give_cols = pl.ds(pl.multiple_of((2 * p + 1 - core) * WIDTH, WIDTH), WIDTH)
        copy = pltpu.make_async_copy(weight.at[:, keep_cols], wbuf.at[p, mine], wloc.at[p])
        copy.start()
        get_w.append(copy)
        start(weight.at[:, give_cols], wbuf.at[p, mine], ws.at[p], wr.at[p], partner)

    get_fwd.wait()

    def transform(block, spec):
        for n in range(0, 2 * SPAN, HALF):
            cols = pl.ds(n, HALF)
            spec[:, cols] = mm(block[...], fwd[0, :, cols]) + mm(block[...], fwd[1, :, cols])

    for k in range(NCTX):
        arrived(rows64(frecv, k), fr.at[k])
    send_signal(1)
    transform(frecv, spec_h)

    def products(off, size):
        for lane in range(4):
            re, im = pl.ds(lane * 128, 128), pl.ds(SPAN + lane * 128, 128)

            @pl.loop(0, size // 8)
            def _(r, re=re, im=im, odd=lane >= 2):
                def taps(d):
                    return pl.ds(pl.multiple_of(d * OWN + off + r * 8, 8), 8)

                def rows(j):
                    return pl.ds(pl.multiple_of(NCTX * off + j * size + r * 8, 8), 8)

                h_re = [spec_h[taps(d), re] for d in range(NCTX)]
                h_im = [spec_h[taps(d), im] for d in range(NCTX)]
                if odd:
                    g_re = [h_re[0]] + [h_re[d] + h_im[d - 1] for d in range(1, NCTX)]
                    g_im = [h_im[0]] + [h_im[d] - h_re[d - 1] for d in range(1, NCTX)]
                else:
                    g_re = [h_re[0]] + [h_re[d] - h_im[d - 1] for d in range(1, NCTX)]
                    g_im = [h_im[0]] + [h_im[d] + h_re[d - 1] for d in range(1, NCTX)]
                x_re = [spec_x[rows(j), re] for j in range(NCTX)]
                x_im = [spec_x[rows(j), im] for j in range(NCTX)]
                for i in range(NCTX):
                    y_re = x_re[0] * g_re[i] - x_im[0] * g_im[i]
                    y_im = x_re[0] * g_im[i] + x_im[0] * g_re[i]
                    for j in range(1, i + 1):
                        y_re = y_re + x_re[j] * g_re[i - j] - x_im[j] * g_im[i - j]
                        y_im = y_im + x_re[j] * g_im[i - j] + x_im[j] * g_re[i - j]
                    spec_y[rows(i), re] = y_re
                    spec_y[rows(i), im] = y_im

        @pl.loop(0, NCTX * size // 32)
        def _(r):
            rows = pl.ds(pl.multiple_of(NCTX * off + r * 32, 32), 32)
            value = spec_y[rows, :]
            high = value.astype(BF)
            yhi[rows, :] = high
            ylo[rows, :] = (value - high.astype(F32)).astype(BF)

    csend, crecv = (csend0, csend1, csend2), (crecv0, crecv1, crecv2)

    def inverse(t, off, size):
        rows, cols = pl.ds(NCTX * off, NCTX * size), pl.ds(*CHUNKS[t])
        back = mm(yhi[rows, :], inv[0, :, cols]) + mm(ylo[rows, :], inv[0, :, cols]) + mm(yhi[rows, :], inv[1, :, cols])
        for i in range(NCTX):
            csend[t][pl.ds(i * OWN + off, size), :] = back[i * size : (i + 1) * size].astype(BF)

    def give_back(t, b, off, size):
        for k, peer in enumerate(peers):
            start(
                rows16(csend[t], peer[0] * OWN + off, size), rows16(crecv[t], c * OWN + off, size),
                cs.at[t, b, k], cr.at[t, b, c], peer,
            )
        pltpu.make_async_copy(
            rows16(csend[t], c * OWN + off, size), rows16(crecv[t], c * OWN + off, size), cr.at[t, b, c]
        ).start()

    get_inv.wait()
    for b, (off, size) in enumerate(BATCHES):
        for k in range(NCTX):
            arrived(rows16(srecv, NCTX * off + k * size, size), sr.at[b, k])
        batch = pl.ds(NCTX * off, NCTX * size)
        transform(srecv.at[batch], spec_x.at[batch])
        products(off, size)
        inverse(0, off, size)
        give_back(0, b, off, size)
    for t in range(1, len(CHUNKS)):
        inverse(t, 0, BATCHES[0][1])
        for off, size in BATCHES[1:]:
            inverse(t, off, size)
        give_back(t, 0, 0, OWN)

    def gate(t):
        for b, (off, size) in enumerate(BATCHES if t == 0 else ((0, OWN),)):
            for k in range(NCTX):
                arrived(rows16(crecv[t], k * OWN + off, size), cr.at[t, b, k])
        rows = pl.ds(*CHUNKS[t])
        conv = nt(eye[: CHUNKS[t][1], : CHUNKS[t][1]], crecv[t][...])
        gated = qbuf[rows, :] * (conv + skip[...] * sbuf[rows, :])
        gbuf[core, rows] = gated.astype(BF)
        start(gbuf.at[core, rows], gbuf.at[core, rows], gs.at[t], gr.at[t], partner)

    def met(t):
        arrived(gbuf.at[1 - core, pl.ds(*CHUNKS[t])], gr.at[t])

    def place(dz, other):
        return ((z + dz) % 4) * 2 + (1 - xh if other else xh)

    def project(t, dz, other, cols):
        p, rows = place(dz, other), pl.ds(*CHUNKS[t])
        return mm(gbuf[0, rows], wbuf[p, :WIDTH, cols]) + mm(gbuf[1, rows], wbuf[p, WIDTH:, cols])

    every, early, late = slice(0, WIDTH), slice(0, EARLY), slice(EARLY, WIDTH)
    z_parts = (
        (0, every, za1, za1r, za2, za2r, zax, zaxr, keep_a),
        (2, early, zb1, zb1r, zb2, zb2r, zbx, zbxr, keep_b),
    )
    x_parts = (
        (1, every, xa, xar, xa1, xa1r, xa2, xa2r, keep_c),
        (2, late, xb, xbr, xb1, xb1r, xb2, xb2r, keep_d),
    )

    def halves(t):
        size = CHUNKS[t][1] // 2
        return pl.ds(0, size), pl.ds(size, size)

    def first(q, o, value):
        t, _, send, recv, *_ = z_parts[q]
        top, low = halves(t)
        send[o] = value.astype(BF)
        start(send.at[o, top], recv.at[0, o], z1s.at[q, 0, o], z1r.at[q, 0, o], up)
        start(send.at[o, low], recv.at[1, o], z1s.at[q, 1, o], z1r.at[q, 1, o], down)

    def second(q, o):
        t, cols, _, had, send, recv, _, _, keep = z_parts[q]
        top, low = halves(t)
        for d, dz, rows, device in ((0, 1, top, up), (1, 3, low, down)):
            keep[...] = project(t, dz, o, cols)
            arrived(had.at[d, o], z1r.at[q, d, o])
            keep[rows, :] += had[d, o].astype(F32)
            send[d, o] = keep[...].astype(BF)
            start(send.at[d, o], recv.at[d, o], z2s.at[q, d, o], z2r.at[q, d, o], device)

    def third(q):
        t, cols, _, _, _, had, send, recv, keep = z_parts[q]
        keep[...] = project(t, 0, 1, cols)
        for d in range(2):
            arrived(had.at[d, 1], z2r.at[q, d, 1])
        send[...] = (keep[...] + had[0, 1].astype(F32) + had[1, 1].astype(F32)).astype(BF)
        start(send, recv, zxs.at[q], zxr.at[q], across)

    def last(q):
        t, cols, _, _, _, had, _, recv, keep = z_parts[q]
        for d in range(2):
            arrived(had.at[d, 0], z2r.at[q, d, 0])
        arrived(recv, zxr.at[q])
        total = keep[...] + had[0, 0].astype(F32) + had[1, 0].astype(F32) + recv[...].astype(F32)
        out[pl.ds(*CHUNKS[t]), cols] = total.astype(BF)

    def over_x(q, dz):
        t, cols, send, recv, *_ = x_parts[q]
        send[dz] = project(t, dz, 1, cols).astype(BF)
        start(send.at[dz], recv.at[dz], xs.at[q, dz], xr.at[q, dz], across)

    def summed(q, dz):
        t, cols, _, had, *_, keep = x_parts[q]
        keep[...] = project(t, dz, 0, cols)
        arrived(had.at[dz], xr.at[q, dz])
        keep[...] += had[dz].astype(F32)

    def apart(q):
        t, _, _, _, send, recv, _, _, keep = x_parts[q]
        top, low = halves(t)
        summed(q, 2)
        send[...] = keep[...].astype(BF)
        start(send.at[top], recv.at[0], s1s.at[q, 0], s1r.at[q, 0], up)
        start(send.at[low], recv.at[1], s1s.at[q, 1], s1r.at[q, 1], down)

    def forward(q):
        t, _, _, _, _, had, send, recv, keep = x_parts[q]
        top, low = halves(t)
        for d, dz, rows, device in ((0, 1, top, up), (1, 3, low, down)):
            summed(q, dz)
            arrived(had.at[d], s1r.at[q, d])
            keep[rows, :] += had[d].astype(F32)
            send[d] = keep[...].astype(BF)
            start(send.at[d], recv.at[d], s2s.at[q, d], s2r.at[q, d], device)

    def close(q):
        t, cols, _, _, _, _, _, had, keep = x_parts[q]
        for d in range(2):
            arrived(had.at[d], s2r.at[q, d])
        out[pl.ds(*CHUNKS[t]), cols] = (keep[...] + had[0].astype(F32) + had[1].astype(F32)).astype(BF)

    gate(0)
    for p in range(8):
        get_w[p].wait()
        arrived(wbuf.at[p, pl.ds(pl.multiple_of((1 - core) * WIDTH, WIDTH), WIDTH)], wr.at[p])
    other, rows = pl.ds(pl.multiple_of((1 - core) * WIDTH, WIDTH), WIDTH), pl.ds(*CHUNKS[0])
    for o, keep in ((1, keep_a), (0, keep_c)):
        keep[...] = mm(gbuf[core, rows], wbuf[place(2, o), mine, :])
    met(0)
    for o, keep in ((1, keep_a), (0, keep_c)):
        first(0, o, keep[...] + mm(gbuf[1 - core, rows], wbuf[place(2, o), other, :]))
    gate(1)
    met(1)
    for dz in (2, 1, 3):
        over_x(0, dz)
    second(0, 1)
    gate(2)
    met(2)
    for o in (1, 0):
        first(1, o, project(2, 2, o, early))
    for dz in (2, 1, 3):
        over_x(1, dz)
    over_x(0, 0)
    over_x(1, 0)
    apart(0)
    third(0)
    second(1, 1)
    apart(1)
    second(0, 0)
    forward(0)
    second(1, 0)
    third(1)
    forward(1)
    for t, cols, *_, keep in z_parts:
        keep[...] = project(t, 0, 0, cols)
    for q in range(2):
        summed(q, 0)
    last(0)
    close(0)
    last(1)
    close(1)
    for copy in sent:
        copy.wait_send()


def per_device(features, short_weight, long_filter, lengths, skip_gain, out_weight):
    forward, inverse = tables()
    dma = pltpu.SemaphoreType.DMA
    vm = pltpu.VMEM
    sizes = [size for _, size in CHUNKS]
    z_shapes = ((sizes[0], WIDTH), (sizes[2], EARLY))
    x_shapes = ((sizes[1], WIDTH), (sizes[2], WIDTH - EARLY))
    scratch = [
        vm((3, 16 + SPAN, WIDTH), BF), vm((16, WIDTH), BF), vm((16, WIDTH), BF),
        vm((SPAN, WIDTH), BF), vm((WIDTH, SPAN), BF), vm((WIDTH, SPAN), BF),
        vm((SPAN, WIDTH), BF), vm((WIDTH, SPAN), BF), vm((WIDTH, SPAN), BF),
        vm((SPAN, WIDTH), F32), vm((SPAN, WIDTH), F32),
        vm((2, SPAN, 2 * SPAN), BF), vm((2, 2 * SPAN, SPAN), BF), vm((HALF, HALF), BF),
        vm((WIDTH, 2 * SPAN), F32), vm((WIDTH, 2 * SPAN), F32), vm((WIDTH, 2 * SPAN), F32),
        vm((WIDTH, 2 * SPAN), BF), vm((WIDTH, 2 * SPAN), BF),
        *[vm((WIDTH, size), BF) for size in sizes], *[vm((WIDTH, size), BF) for size in sizes],
        vm((2, SPAN, WIDTH), BF), vm((8, 2 * WIDTH, WIDTH), BF),
    ]
    for rows, cols in z_shapes:
        scratch += [
            vm((2, rows, cols), BF), vm((2, 2, rows // 2, cols), BF),
            vm((2, 2, rows, cols), BF), vm((2, 2, rows, cols), BF),
            vm((rows, cols), BF), vm((rows, cols), BF),
        ]
    for rows, cols in x_shapes:
        scratch += [
            vm((4, rows, cols), BF), vm((4, rows, cols), BF),
            vm((rows, cols), BF), vm((2, rows // 2, cols), BF),
            vm((2, rows, cols), BF), vm((2, rows, cols), BF),
        ]
    scratch += [
        *[vm(shape, F32) for shape in z_shapes + x_shapes],
        dma((4,)), dma((8,)), dma((1,)), dma((1,)),
        dma((7,)), dma((8,)), dma((2, 7)), dma((2, 8)), dma((8,)), dma((8,)),
        dma((3, 2, 7)), dma((3, 2, 8)), dma((3,)), dma((3,)),
        dma((2, 4)), dma((2, 4)), dma((2, 2, 2)), dma((2, 2, 2)), dma((2, 2, 2)), dma((2, 2, 2)),
        dma((2,)), dma((2,)), dma((2, 2)), dma((2, 2)), dma((2, 2)), dma((2, 2)),
    ]
    hbm = pl.BlockSpec(memory_space=pl.ANY)
    near = pl.BlockSpec(memory_space=pltpu.VMEM)
    return pl.pallas_call(
        kernel,
        out_shape=jax.ShapeDtypeStruct((SPAN, WIDTH), BF),
        in_specs=[pl.BlockSpec(memory_space=pltpu.SMEM), near, near, hbm, hbm, hbm, hbm, hbm],
        out_specs=near,
        scratch_shapes=scratch,
        name="hyena",
        compiler_params=pltpu.CompilerParams(
            collective_id=0, has_side_effects=True, vmem_limit_bytes=56 * 2**20
        ),
    )(
        lengths, short_weight, skip_gain.reshape(1, WIDTH), features, long_filter, out_weight,
        jnp.asarray(forward), jnp.asarray(inverse),
    )


def solution(mesh):
    return jax.shard_map(
        per_device,
        mesh=mesh,
        in_specs=(
            P(None, "ctx", "grp"),
            P(None, None, "grp"),
            P("ctx", "grp"),
            P(),
            P("grp"),
            P("grp", None),
        ),
        out_specs=P("ctx", "grp"),
        check_vma=False,
    )
```

time: 67.7 us -> 65.6 us (0.969)
  Pallas kernels: 65.6 us -> 63.2 us
    pallas_call x1, Pallas kernels: 65.6 us -> 63.2 us  [per_device(): pl.pallas_call(kernel, out_shape=jax.ShapeDtypeStruct((SPAN, WIDTH), BF),...]
where the time goes in v3:
time: 65.6 us; the launch traced here: 65.1 us
  Pallas kernels  63.2 us (96%)
  local copies, waits for them, and re-layouts  1.87 us (3%)
    pallas_call x1, Pallas kernels, per_device(): pl.pallas_call(kernel, out_shape=jax.ShapeDtypeStruct((SPAN, WIDTH), BF),...  63.2 us
    unnamed x1, local copies, waits for them, and re-layouts  1.87 us

profile of v3, /device:TPU:0, one launch (start us, length us, event | category | flops | bytes accessed | tf_op | source)
XLA Modules:
  0.0 65.1 jit_solution(1430312501613852184)
XLA Ops:
  0.0 63.2 %hyena.1 = bf16[512,512]{1,0:T(8,128)(2,1)} custom-call(s32[32]{0:T(128)} %lens.1, f32[3,3,512]{2,1,0:T(4,128)} %sw.1, f32[1,512]{1,0:T(1,128)} %bitcast.1, bf16[3,512,512]{2,1,0:T(8,128)(2,1)} %feat.1, bf16[512,512]{1,0:T(8,128)(2,1)} %filt.1, bf16[512,8192]{1,0:T(8,128)(2,1)} %weight.1, bf16[2,512,1024]{2,1,0:T(8,128)(2,1)} %constant.4.clone.fwd_hbm, ...), custom_call_target="tpu_custom_call" | custom-call | tf_op jit(solution)/shard_map/hyena/pallas_call | solution.py:446
  63.2 1.9 %copy.10 = bf16[512,512]{1,0:T(8,128)(2,1)} copy(bf16[512,512]{1,0:T(8,128)(2,1)} %hyena.1) | data formatting | bytes 1048576

commit v4 on v3

--- a/solution.py
+++ b/solution.py
@@ -44,9 +44,9 @@
 
 
 def kernel(
-    lens, sw, skip, feat, filt, weight, fwd_hbm, inv_hbm,
+    lens_hbm, sw_hbm, skip_hbm, feat, filt, weight, fwd_hbm, inv_hbm,
     out,
-    ext, edge, halo, ftmp, fsend, frecv, sbf, ssend, srecv, qbuf, sbuf, fwd, inv, eye,
+    lens, sw, skip, ext, edge, halo, ftmp, fsend, frecv, sbf, ssend, srecv, qbuf, sbuf, fwd, inv, eye,
     spec_h, spec_x, spec_y, yhi, ylo, csend0, csend1, csend2, crecv0, crecv1, crecv2, gbuf, wbuf,
     za1, za1r, za2, za2r, zax, zaxr, zb1, zb1r, zb2, zb2r, zbx, zbxr,
     xa, xar, xa1, xa1r, xa2, xa2r, xb, xbr, xb1, xb1r, xb2, xb2r, keep_a, keep_b, keep_c, keep_d,
@@ -82,24 +82,31 @@
     def rows16(ref, base, size):
         return ref.at[pl.ds(pl.multiple_of(base, 16), size)]
 
+    barrier = pltpu.get_barrier_semaphore()
+    peers = [(lax.rem(c + k, NCTX), g) for k in range(1, NCTX)]
+    for device in peers + [partner, across, up, down]:
+        pl.semaphore_signal(barrier, inc=1, device_id=device, device_id_type=MESH)
+
     get_filt = pltpu.make_async_copy(filt, ftmp, loc.at[0])
     get_feat = pltpu.make_async_copy(feat, ext.at[:, pl.ds(16, SPAN)], loc.at[1])
     get_fwd = pltpu.make_async_copy(fwd_hbm, fwd, loc.at[2])
     get_inv = pltpu.make_async_copy(inv_hbm, inv, loc.at[3])
+    get_lens = pltpu.make_async_copy(lens_hbm, lens, loc.at[4])
+    get_sw = pltpu.make_async_copy(sw_hbm, sw, loc.at[5])
+    get_skip = pltpu.make_async_copy(skip_hbm, skip, loc.at[6])
+    get_lens.start()
     get_filt.start()
     get_feat.start()
+    get_sw.start()
+    get_skip.start()
     get_fwd.start()
     get_inv.start()
     mine = pl.ds(pl.multiple_of(core * WIDTH, WIDTH), WIDTH)
 
-    barrier = pltpu.get_barrier_semaphore()
-    peers = [(lax.rem(c + k, NCTX), g) for k in range(1, NCTX)]
-    for device in peers + [partner, across, up, down]:
-        pl.semaphore_signal(barrier, inc=1, device_id=device, device_id_type=MESH)
-
     eye[...] = (
         lax.broadcasted_iota(jnp.int32, (HALF, HALF), 0) == lax.broadcasted_iota(jnp.int32, (HALF, HALF), 1)
     ).astype(F32).astype(BF)
+    get_lens.wait()
     get_filt.wait()
     for part in range(WIDTH // GROUP_CH):
         length = lens[2 * g + part]
@@ -138,6 +145,9 @@
         signal = res[1] * res[2]
         sbuf[here, :] = signal
         sbf[here, :] = signal.astype(BF)
+
+    get_sw.wait()
+    get_skip.wait()
 
     @pl.loop(1, SPAN // 32)
     def _(block):
@@ -163,6 +173,7 @@
         ).start()
 
     send_signal(0)
+    send_signal(1)
 
     get_w = []
     for p in range(8):
@@ -182,7 +193,6 @@
 
     for k in range(NCTX):
         arrived(rows64(frecv, k), fr.at[k])
-    send_signal(1)
     transform(frecv, spec_h)
 
     def products(off, size):
@@ -411,6 +421,7 @@
     z_shapes = ((sizes[0], WIDTH), (sizes[2], EARLY))
     x_shapes = ((sizes[1], WIDTH), (sizes[2], WIDTH - EARLY))
     scratch = [
+        pltpu.SMEM((32,), jnp.int32), vm((3, 3, WIDTH), F32), vm((1, WIDTH), F32),
         vm((3, 16 + SPAN, WIDTH), BF), vm((16, WIDTH), BF), vm((16, WIDTH), BF),
         vm((SPAN, WIDTH), BF), vm((WIDTH, SPAN), BF), vm((WIDTH, SPAN), BF),
         vm((SPAN, WIDTH), BF), vm((WIDTH, SPAN), BF), vm((WIDTH, SPAN), BF),
@@ -435,7 +446,7 @@
         ]
     scratch += [
         *[vm(shape, F32) for shape in z_shapes + x_shapes],
-        dma((4,)), dma((8,)), dma((1,)), dma((1,)),
+        dma((7,)), dma((8,)), dma((1,)), dma((1,)),
         dma((7,)), dma((8,)), dma((2, 7)), dma((2, 8)), dma((8,)), dma((8,)),
         dma((3, 2, 7)), dma((3, 2, 8)), dma((3,)), dma((3,)),
         dma((2, 4)), dma((2, 4)), dma((2, 2, 2)), dma((2, 2, 2)), dma((2, 2, 2)), dma((2, 2, 2)),
@@ -445,8 +456,8 @@
     near = pl.BlockSpec(memory_space=pltpu.VMEM)
     return pl.pallas_call(
         kernel,
-        out_shape=jax.ShapeDtypeStruct((SPAN, WIDTH), BF),
-        in_specs=[pl.BlockSpec(memory_space=pltpu.SMEM), near, near, hbm, hbm, hbm, hbm, hbm],
+        out_shape=pltpu.VMEM((SPAN, WIDTH), BF),
+        in_specs=[hbm] * 8,
         out_specs=near,
         scratch_shapes=scratch,
         name="hyena",

time: 65.6 us -> 62.6 us (0.954)
  Pallas kernels: 63.2 us -> 61.4 us
  local copies, waits for them, and re-layouts: 1.87 us -> 0.8 us
    pallas_call x1, Pallas kernels: 63.2 us -> 61.4 us  [per_device(): pl.pallas_call(kernel, out_shape=pltpu.VMEM((SPAN, WIDTH), BF), in_specs=...]
    unnamed x1, local copies, waits for them, and re-layouts: 1.87 us -> 0.8 us
where the time goes in v4:
time: 62.6 us; the launch traced here: 62.2 us
  Pallas kernels  61.4 us (98%)
  local copies, waits for them, and re-layouts  0.8 us (1%)
    pallas_call x1, Pallas kernels, per_device(): pl.pallas_call(kernel, out_shape=pltpu.VMEM((SPAN, WIDTH), BF), in_specs=...  61.4 us

profile of v4, /device:TPU:0, one launch (start us, length us, event | category | flops | bytes accessed | tf_op | source)
XLA Modules:
  0.0 62.2 jit_solution(10387231449700012244)
XLA Ops:
  0.0 61.4 %hyena.1 = bf16[512,512]{1,0:T(8,128)(2,1)S(1)} custom-call(s32[32]{0:T(128)} %lens_hbm.1, f32[3,3,512]{2,1,0:T(4,128)} %sw_hbm.1, f32[1,512]{1,0:T(1,128)} %bitcast.1, bf16[3,512,512]{2,1,0:T(8,128)(2,1)} %feat.1, bf16[512,512]{1,0:T(8,128)(2,1)} %filt.1, bf16[512,8192]{1,0:T(8,128)(2,1)} %weight.1, bf16[2,512,1024]{2,1,0:T(8,128)(2,1)} %constant.4.clone.fwd_hbm, ...), custom_call_target="tpu_custom_call" | custom-call | tf_op jit(solution)/shard_map/hyena/pallas_call | solution.py:457
  61.4 0.8 %copy.10 = bf16[512,512]{1,0:T(8,128)(2,1)} copy(bf16[512,512]{1,0:T(8,128)(2,1)S(1)} %hyena.1) | data formatting | bytes 1048576

commit v5 on v4

--- a/solution.py
+++ b/solution.py
@@ -73,6 +73,11 @@
         sent.append(copy)
         return copy
 
+    def drain(copies):
+        for copy in copies:
+            copy.wait_send()
+        copies.clear()
+
     def arrived(dst, recv):
         remote(dst, dst, hs.at[0], recv, partner).wait_recv()
 
@@ -143,7 +148,7 @@
             res.append(acc)
         qbuf[here, :] = res[0]
         signal = res[1] * res[2]
-        sbuf[here, :] = signal
+        sbuf[here, :] = res[0] * (skip[...] * signal)
         sbf[here, :] = signal.astype(BF)
 
     get_sw.wait()
@@ -273,7 +278,7 @@
                 arrived(rows16(crecv[t], k * OWN + off, size), cr.at[t, b, k])
         rows = pl.ds(*CHUNKS[t])
         conv = nt(eye[: CHUNKS[t][1], : CHUNKS[t][1]], crecv[t][...])
-        gated = qbuf[rows, :] * (conv + skip[...] * sbuf[rows, :])
+        gated = qbuf[rows, :] * conv + sbuf[rows, :]
         gbuf[core, rows] = gated.astype(BF)
         start(gbuf.at[core, rows], gbuf.at[core, rows], gs.at[t], gr.at[t], partner)
 
@@ -369,10 +374,12 @@
             arrived(had.at[d], s2r.at[q, d])
         out[pl.ds(*CHUNKS[t]), cols] = (keep[...] + had[0].astype(F32) + had[1].astype(F32)).astype(BF)
 
-    gate(0)
     for p in range(8):
         get_w[p].wait()
         arrived(wbuf.at[p, pl.ds(pl.multiple_of((1 - core) * WIDTH, WIDTH), WIDTH)], wr.at[p])
+    gate(0)
+    before = sent[:]
+    sent.clear()
     other, rows = pl.ds(pl.multiple_of((1 - core) * WIDTH, WIDTH), WIDTH), pl.ds(*CHUNKS[0])
     for o, keep in ((1, keep_a), (0, keep_c)):
         keep[...] = mm(gbuf[core, rows], wbuf[place(2, o), mine, :])
@@ -395,9 +402,12 @@
     apart(0)
     third(0)
     second(1, 1)
+    drain(before)
     apart(1)
     second(0, 0)
     forward(0)
+    before = sent[:-6]
+    del sent[:-6]
     second(1, 0)
     third(1)
     forward(1)
@@ -405,12 +415,12 @@
         keep[...] = project(t, 0, 0, cols)
     for q in range(2):
         summed(q, 0)
+    drain(before)
     last(0)
     close(0)
     last(1)
     close(1)
-    for copy in sent:
-        copy.wait_send()
+    drain(sent)
 
 
 def per_device(features, short_weight, long_filter, lengths, skip_gain, out_weight):

time: 62.6 us -> 62.5 us (level)
  no operation moved by 1% of the time
where the time goes in v5:
time: 62.5 us; the launch traced here: 62.1 us
  Pallas kernels  61.3 us (98%)
  local copies, waits for them, and re-layouts  0.8 us (1%)
    pallas_call x1, Pallas kernels, per_device(): pl.pallas_call(kernel, out_shape=pltpu.VMEM((SPAN, WIDTH), BF), in_specs=...  61.3 us

profile of v5, /device:TPU:0, one launch (start us, length us, event | category | flops | bytes accessed | tf_op | source)
XLA Modules:
  0.0 62.1 jit_solution(13999095932632819672)
XLA Ops:
  0.0 61.3 %hyena.1 = bf16[512,512]{1,0:T(8,128)(2,1)S(1)} custom-call(s32[32]{0:T(128)} %lens_hbm.1, f32[3,3,512]{2,1,0:T(4,128)} %sw_hbm.1, f32[1,512]{1,0:T(1,128)} %bitcast.1, bf16[3,512,512]{2,1,0:T(8,128)(2,1)} %feat.1, bf16[512,512]{1,0:T(8,128)(2,1)} %filt.1, bf16[512,8192]{1,0:T(8,128)(2,1)} %weight.1, bf16[2,512,1024]{2,1,0:T(8,128)(2,1)} %constant.4.clone.fwd_hbm, ...), custom_call_target="tpu_custom_call" | custom-call | tf_op jit(solution)/shard_map/hyena/pallas_call | solution.py:467
  61.3 0.8 %copy.10 = bf16[512,512]{1,0:T(8,128)(2,1)} copy(bf16[512,512]{1,0:T(8,128)(2,1)S(1)} %hyena.1) | data formatting | bytes 1048576
